TPU v7x, 32 devices: a whole 2x2x4 slice. The times are simulated.
32 devices in a mesh: section: 2 (over core), ctx: 16 (over z, y, x).
Axes of the slice: x: 2, y: 2, z: 4, core: 2. Of those that a mesh axis runs over, the one named last changes fastest.
Arguments:
- tokens: bfloat16 [2, 2048, 1024], P(None, 'ctx'), may hold values from -6 to 6
- cotangent: bfloat16 [2, 2048, 1024], P(None, 'ctx'), may hold values from -6 to 6
- bounds: int32 [2, 8], replicated, may hold values from 0 to 2048, as said below
- norm_gain: bfloat16 [2, 1024], P('section'), may hold values from 0.5 to 1.5
- in_proj: bfloat16 [2, 1024, 4096], P('section'), may hold values from -0.1875 to 0.1875
- conv_kernel: bfloat16 [2, 4, 2048], P('section'), may hold values from -3 to 3
- conv_bias: bfloat16 [2, 2048], P('section'), may hold values from -3 to 3
- x_proj: bfloat16 [2, 2048, 96], P('section'), may hold values from -0.125 to 0.125
- dt_proj: bfloat16 [2, 64, 2048], P('section'), may hold values from -0.75 to 0.75
- dt_bias: bfloat16 [2, 2048], P('section'), may hold values from -9 to 1
- skip_gain: bfloat16 [2, 2048], P('section'), may hold values from 0.5 to 1.5
- out_proj: bfloat16 [2, 2048, 1024], P('section'), may hold values from -0.25 to 0.25
Outputs:
- block_out: bfloat16 [2, 2048, 1024], P('section', 'ctx')
- grad_tokens: bfloat16 [2, 2048, 1024], P('section', 'ctx')
- grad_norm_gain: float32 [2, 1024], P('section', 'ctx')
- grad_in_proj: float32 [2, 1024, 4096], P('section', 'ctx')
- grad_conv_kernel: float32 [2, 4, 2048], P('section', None, 'ctx')
- grad_conv_bias: float32 [2, 2048], P('section', 'ctx')
- grad_x_proj: float32 [2, 2048, 96], P('section', 'ctx')
- grad_dt_proj: float32 [2, 64, 2048], P('section', 'ctx')
- grad_dt_bias: float32 [2, 2048], P('section', 'ctx')
- grad_skip_gain: float32 [2, 2048], P('section', 'ctx')
- grad_out_proj: float32 [2, 2048, 1024], P('section', 'ctx')
Inputs may be any that keep to these rules, and one draw needn't show every extreme that they name: Each row bounds[m] rises strictly from 0 to 2048: seven sequences. In one micro-batch, chosen by the draw, the first three sequences end within the first 128 tokens and the last three start within the last 128 tokens. In every other micro-batch the cuts lie anywhere, and the sequences are four of 128 tokens and three of 512 tokens in some order, with the first one longer and the last one shorter by the same amount, less than 64.
All inputs are finite; a program needn't handle non-finite values.
Results may differ from a plain program's by a relative error of at most 0.023.
Values may be sent and summed in bfloat16 or wider, within the bound.
A program may use at most 256 MiB of HBM per device.

v0:
```python
import functools
import math

import jax
import jax.numpy as jnp
from jax import lax
from jax.experimental import pallas as pl
from jax.experimental.pallas import tpu as pltpu
from jax.sharding import PartitionSpec as P

NORM_EPS = 1e-05
LOG2E = math.log2(math.e)
BF = jnp.bfloat16
F32 = jnp.float32
MESH = pl.DeviceIdType.MESH
LANES = 128
BT = 16
N = 16
MIB = 2**20
VSPEC = pl.BlockSpec(memory_space=pltpu.VMEM)
ANYSPEC = pl.BlockSpec(memory_space=pl.ANY)


def dot(a, b):
    return jnp.dot(a, b, preferred_element_type=F32)


def dot_nt(a, b):
    return lax.dot_general(a, b, (((1,), (1,)), ((), ())), preferred_element_type=F32)


def dot_tn(a, b):
    return lax.dot_general(a, b, (((0,), (0,)), ((), ())), preferred_element_type=F32)


def iota(shape, dim):
    return lax.broadcasted_iota(jnp.int32, shape, dim)


def silu_parts(v):
    s = jax.nn.sigmoid(v)
    return v * s, s * (1.0 + v * (1.0 - s))


def coords(n):
    bits = n.bit_length() - 1
    me = lax.axis_index("ctx")
    return bits, me, [lax.rem(me // 2**b, 2) for b in range(bits)]


def unpack_index(k, dims):
    return tuple(lax.rem(k // 2 ** (dims - 1 - d), 2) for d in range(dims))


class Carry:
    def __init__(self, sec, me, n, src, recv, pre, dst, sems, decay, inner):
        self.sec, self.me, self.n = sec, me, n
        self.src, self.recv, self.pre, self.dst, self.decay = src, recv, pre, dst, decay
        self.send1, self.recv1, self.send2, self.recv2 = sems
        self.blocks = min(n, inner // LANES)
        self.stride = n // self.blocks
        self.mine = me // self.stride
        self.reverse = decay is not None

    def when(self, cond, fn):
        if self.stride == 1:
            fn()
        else:
            pl.when(cond)(fn)

    def to(self, k):
        return lax.rem(self.me + k, self.n)

    def frm(self, k):
        return lax.rem(self.me - k + self.n, self.n)

    def lane(self, dev):
        return pl.ds(pl.multiple_of((dev // self.stride) * LANES, LANES), LANES)

    def owns(self, dev):
        return lax.rem(dev, self.stride) == 0

    def first(self, k, dev, slot):
        return pltpu.make_async_remote_copy(
            src_ref=self.src.at[:, self.lane(dev)], dst_ref=self.recv.at[slot],
            send_sem=self.send1.at[k], recv_sem=self.recv1.at[slot],
            device_id=(self.sec, dev), device_id_type=MESH)

    def second(self, k, dev, frm):
        return pltpu.make_async_remote_copy(
            src_ref=self.pre.at[dev], dst_ref=self.dst.at[:, self.lane(frm)],
            send_sem=self.send2.at[k], recv_sem=self.recv2.at[frm],
            device_id=(self.sec, dev), device_id_type=MESH)

    def send(self):
        for k in range(1, self.n):
            self.when(self.owns(self.to(k)), lambda k=k: self.first(k, self.to(k), self.me).start())

    def combine(self):
        def own():
            self.recv[self.me] = self.src[:, self.lane(self.me)]
            for k in range(1, self.n):
                self.first(k, self.frm(k), self.frm(k)).wait_recv()
            run = jnp.zeros((N, LANES), F32)
            for i in range(self.n):
                d = self.n - 1 - i if self.reverse else i
                self.pre[d] = run.astype(BF)
                if self.reverse:
                    dec, st = self.decay[d], self.recv[d]
                else:
                    dec, st = self.recv[d, 0:N, :], self.recv[d, N : 2 * N, :]
                    self.decay_out[d] = dec
                run = dec.astype(F32) * run + st.astype(F32)
            for k in range(1, self.n):
                self.second(k, self.to(k), self.me).start()
            self.dst[:, self.lane(self.me)] = self.pre[self.me]

        self.when(self.owns(self.me), own)

    def get(self):
        for k in range(1, self.n):
            self.when(
                self.owns(self.frm(k)),
                lambda k=k: pltpu.make_async_remote_copy(
                    src_ref=self.pre.at[0], dst_ref=self.dst.at[:, self.lane(self.frm(k))],
                    send_sem=self.send2.at[k], recv_sem=self.recv2.at[self.frm(k)],
                    device_id=(self.sec, self.frm(k)), device_id_type=MESH).wait_recv())

    def sent(self):
        for k in range(1, self.n):
            self.when(self.owns(self.to(k)), lambda k=k: self.first(k, self.to(k), self.me).wait_send())

        def own():
            for k in range(1, self.n):
                self.second(k, self.to(k), self.me).wait_send()

        self.when(self.owns(self.me), own)


SAVED = ("xi", "z", "c", "beta", "ex", "us", "k2", "qb", "y", "proj", "dec", "sb")


def block_diag(projb, first_col):
    pick = (iota((LANES, BT * N), 0) == first_col + iota((LANES, BT * N), 1) % N).astype(F32).astype(BF)
    vals = dot(projb, pick)
    same = iota((BT, BT * N), 0) == iota((BT, BT * N), 1) // N
    return jnp.where(same, vals, 0.0)


def forward_kernel(n, rank, *refs):
    refs = list(refs)

    def take(k):
        out = refs[:k]
        del refs[:k]
        return out

    bounds_ref, tok_ref, gain_ref, ck_ref, cb_ref, dtb_ref, skip_ref, xproj_ref, dtproj_ref, in_own, out_own = take(11)
    in_oth, out_oth, mask_ref, xp2, dtp2, vec2, hmid_ref, hout_ref = take(8)
    hbm = [dict(zip(SAVED + ("s", "ut4", "ot4"), take(len(SAVED) + 3))) for _ in range(2)]
    loc = dict(zip(SAVED, take(len(SAVED))))
    kb_ref, w_in, w_out, stage, rim_ref, hrow, st, sbuf, o_all, ut_s, ot_s = take(11)
    c_src, c_recv, c_pre, c_dst = take(4)
    (sv_sem, wi_sem, wo_sem, sm_s, sm_r, xz_s, xz_r, oth_s, oth_r, rim_s, rim_r, s_sem, op_s, op_r, own_sem,
     c1, c2, c3, c4) = take(19)
    assert not refs
    sec = lax.axis_index("section")
    bits, me, mybit = coords(n)
    x = mybit[0]
    neigh = me + 1 - 2 * x
    t_len, width = hout_ref.shape
    inner = w_out.shape[0]
    used = xproj_ref.shape[1]
    cb = 512
    n_half = inner // cb
    rim = rim_ref.shape[2]
    barrier = pltpu.get_barrier_semaphore()
    for k in range(1, n):
        pl.semaphore_signal(barrier, inc=1, device_id=(sec, lax.rem(me + k, n)), device_id_type=MESH)
    pl.semaphore_signal(barrier, inc=1, device_id=(1 - sec, me), device_id_type=MESH)

    in_order = list(range(n_half, 2 * n_half)) + list(range(n_half))

    def in_copy(k, src):
        at = pl.ds(k * cb, cb)
        return pltpu.make_async_copy(src.at[:, at], w_in.at[:, at], wi_sem.at[k])

    def out_copy(src):
        return pltpu.make_async_copy(src, w_out, wo_sem)

    @pl.when(sec == 0)
    def _():
        for k in in_order:
            in_copy(k, in_own).start()
        out_copy(out_own).start()

    @pl.when(sec == 1)
    def _():
        for k in in_order:
            in_copy(k, in_own).start()

    vec2[sec, 0:4, :] = ck_ref[...].astype(F32)
    vec2[sec, 4:5, :] = cb_ref[...].astype(F32)
    vec2[sec, 5:6, :] = dtb_ref[...].astype(F32)
    vec2[sec, 6:7, :] = skip_ref[...].astype(F32)
    vec2[sec, 7:8, 0:width] = gain_ref[...].astype(F32)
    vec2[sec, 7:8, width:inner] = jnp.zeros((1, inner - width), F32)
    xp2[sec, :, :] = jnp.concatenate([xproj_ref[...], jnp.zeros((inner, LANES - used), BF)], axis=1)
    dtp2[sec, 0:rank, :] = dtproj_ref[...]
    dtp2[sec, rank:LANES, :] = jnp.zeros((LANES - rank, inner), BF)
    row = me * t_len + iota((t_len, LANES), 0)
    col = iota((t_len, LANES), 1)
    start = jnp.zeros((t_len, LANES), jnp.int32)
    for cut in range(1, 7):
        bound = bounds_ref[sec, cut]
        start = jnp.where(row >= bound, bound, start)
    tap = jnp.where(row - 3 + col >= start, 1.0, 0.0)
    keeps = jnp.where(row != start, 1.0, 0.0)
    mask_ref[...] = jnp.where(col < 4, tap, jnp.where(col == 4, keeps, 0.0))

    pl.semaphore_wait(barrier, n)

    def sibling(src, dst, a, b):
        return pltpu.make_async_remote_copy(
            src_ref=src, dst_ref=dst, send_sem=a, recv_sem=b, device_id=(1 - sec, me), device_id_type=MESH)

    small = [sibling(r.at[sec], r.at[sec], sm_s.at[i], sm_r.at[i]) for i, r in enumerate((vec2, xp2, dtp2))]
    for cp in small:
        cp.start()

    def rim_copy(layer, to):
        src = tok_ref.at[:, pl.ds(t_len - rim, rim), :] if layer == 0 else hrow.at[pl.ds(t_len - rim, rim), :]
        dst = rim_ref.at[0] if layer == 0 else rim_ref.at[1, 0]
        return pltpu.make_async_remote_copy(
            src_ref=src, dst_ref=dst, send_sem=rim_s.at[layer], recv_sem=rim_r.at[layer],
            device_id=(sec, to), device_id_type=MESH)

    def has_rim(layer, cond):
        return cond & (sec == 0) if layer == 0 else cond

    def send_rim(layer):
        @pl.when(has_rim(layer, me < n - 1))
        def _():
            rim_copy(layer, me + 1).start()

        @pl.when(me == 0)
        def _():
            if layer == 0:
                rim_ref[0] = jnp.zeros(rim_ref.shape[1:], BF)
            else:
                rim_ref[1, 0] = jnp.zeros(rim_ref.shape[2:], BF)

    def get_rim(layer):
        @pl.when(has_rim(layer, me > 0))
        def _():
            rim_copy(layer, me).wait_recv()

    send_rim(0)

    def xz_copy(k, rows):
        at = pl.ds((k % n_half) * cb, cb)
        dst = loc["z"] if k >= n_half else loc["xi"]
        return sibling(stage.at[k, pl.ds(0, rows), :], dst.at[:, at], xz_s.at[k], xz_r.at[k])

    def oth(k):
        if k == 0:
            return sibling(out_own, out_oth, oth_s.at[0], oth_r.at[0])
        return sibling(in_own, in_oth, oth_s.at[1], oth_r.at[1])

    def normed(h, layer):
        hf = h.astype(F32)
        inv = lax.rsqrt(jnp.mean(hf * hf, axis=-1, keepdims=True) + NORM_EPS)
        return (hf * inv * vec2[layer, 7:8, 0:width]).astype(BF)

    @pl.when(sec == 0)
    def _():
        both = normed(jnp.concatenate([tok_ref[0], tok_ref[1]], axis=0), 0)
        for k in in_order[:n_half]:
            in_copy(k, in_own).wait()
            r = dot(both, w_in[:, k * cb : (k + 1) * cb])
            loc["z"][:, pl.ds((k - n_half) * cb, cb)] = r[:t_len]
            stage[k, 0:t_len, :] = r[t_len:]
            xz_copy(k, t_len).start()
        get_rim(0)
        edge = normed(jnp.concatenate([rim_ref[0, 0], rim_ref[0, 1]], axis=0), 0)
        rows = jnp.concatenate([edge[:rim], both[:t_len], edge[rim:], both[t_len:]], axis=0)
        for k in in_order[n_half:]:
            in_copy(k, in_own).wait()
            r = dot(rows, w_in[:, k * cb : (k + 1) * cb])
            loc["xi"][:, pl.ds(k * cb, cb)] = r[: rim + t_len]
            stage[k] = r[rim + t_len :]
            xz_copy(k, rim + t_len).start()

    hrow[...] = tok_ref[sec]
    for cp in small:
        cp.wait_recv()

    @pl.when(sec == 1)
    def _():
        for k in in_order:
            xz_copy(k, t_len if k >= n_half else rim + t_len).wait_recv()

    oth(0).start()
    oth(1).start()

    carries = []
    saved = []

    def keep(name, layer):
        cp = pltpu.make_async_copy(loc[name], hbm[layer][name], sv_sem.at[layer, SAVED.index(name)])
        cp.start()
        saved.append((layer, name))

    def kept(name, layer):
        pltpu.make_async_copy(loc[name], hbm[layer][name], sv_sem.at[layer, SAVED.index(name)]).wait()

    def part_copy(kind, layer, k, where_from, where_to):
        src = (ut_s, ot_s)[kind].at[layer]
        dst = hbm[layer][("ut4", "ot4")[kind]]

        def slot(i):
            return pl.ds(pl.multiple_of(i * t_len, LANES), t_len)

        mine = 2 * sec + x
        if k == 0:
            s, i, to = src.at[:, x], mine, (1 - sec, me)
        elif k == 1:
            s, i, to = src.at[:, 1 - x], mine, (sec, neigh)
        else:
            i, to = 2 * sec + 1 - x, (1 - sec, me)
            s = dst.at[:, :, slot(i)]
        return pltpu.make_async_remote_copy(
            src_ref=s, dst_ref=dst.at[:, :, slot(i)], send_sem=op_s.at[layer, kind, k], recv_sem=op_r.at[layer, kind, i],
            device_id=to, device_id_type=MESH)

    def part_arrived(kind, layer, i):
        dst = hbm[layer][("ut4", "ot4")[kind]]
        at = pl.ds(pl.multiple_of(i * t_len, LANES), t_len)
        pltpu.make_async_remote_copy(
            src_ref=(ut_s, ot_s)[kind].at[layer, :, 0], dst_ref=dst.at[:, :, at], send_sem=op_s.at[layer, kind, 0],
            recv_sem=op_r.at[layer, kind, i], device_id=(1 - sec, me), device_id_type=MESH).wait_recv()

    def part_own(kind, layer):
        at = pl.ds(pl.multiple_of((2 * sec + x) * t_len, LANES), t_len)
        return pltpu.make_async_copy(
            (ut_s, ot_s)[kind].at[layer, :, x], hbm[layer][("ut4", "ot4")[kind]].at[:, :, at], own_sem.at[layer, kind])

    def part_send(kind, layer):
        part_copy(kind, layer, 0, None, None).start()
        part_copy(kind, layer, 1, None, None).start()
        part_own(kind, layer).start()

    def part_forward(kind, layer):
        part_arrived(kind, layer, 2 * sec + 1 - x)
        part_copy(kind, layer, 2, None, None).start()

    mask = mask_ref[...]
    cols = iota((t_len, LANES), 1)
    keepc = mask[:, 4:5]
    for layer in range(2):
        vec, xp, dtp = vec2.at[layer], xp2.at[layer], dtp2.at[layer]
        u = normed(hrow[...], layer)
        if layer == 1:
            for k in in_order[:n_half]:
                in_copy(k, in_own).wait()
                loc["z"][:, pl.ds((k - n_half) * cb, cb)] = dot(u, w_in[:, k * cb : (k + 1) * cb])
            get_rim(1)
            rows = jnp.concatenate([normed(rim_ref[1, 0], 1), u], axis=0)
            for k in in_order[n_half:]:
                in_copy(k, in_own).wait()
                loc["xi"][:, pl.ds(k * cb, cb)] = dot(rows, w_in[:, k * cb : (k + 1) * cb])
        keep("z", layer)
        keep("xi", layer)
        proj = jnp.zeros((t_len, LANES), F32)
        for k in range(n_half):
            at = pl.ds(k * cb, cb)
            xi = loc["xi"][:, at]
            c = vec[4:5, at] + vec[3:4, at] * xi[rim:]
            for j in range(3):
                c = c + vec[j : j + 1, at] * xi[rim - 3 + j : rim - 3 + j + t_len] * mask[:, j : j + 1]
            loc["c"][:, at] = c
            xc = c * jax.nn.sigmoid(c)
            loc["us"][:, at] = xc
            proj = proj + dot(xc.astype(BF), xp[at, :])
        keep("c", layer)
        projb = jnp.where(cols == rank + 2 * N, keepc, proj).astype(BF)
        loc["proj"][...] = projb
        keep("proj", layer)
        pf = projb.astype(F32)
        ksum = jnp.sum(jnp.where((cols >= rank) & (cols < rank + N), pf * pf, 0.0), axis=-1, keepdims=True)
        for k in range(n_half):
            at = pl.ds(k * cb, cb)
            beta = jax.nn.sigmoid(dot(projb, dtp[:, at]) + vec[5:6, at])
            eps = beta / (1.0 + beta * ksum)
            loc["beta"][:, at] = beta
            loc["us"][:, at] = loc["us"][:, at] * eps
            loc["ex"][:, at] = jnp.where(keepc > 0.0, eps, 1.0)
        for name in ("beta", "us", "ex"):
            keep(name, layer)
        nrow = t_len * N
        sel = (iota((nrow, t_len), 0) // N == iota((nrow, t_len), 1)).astype(F32).astype(BF)
        spread = dot(sel, projb).astype(BF)
        rn = iota((nrow, LANES), 0) % N
        cl = iota((nrow, LANES), 1)
        ones = jnp.ones((LANES, LANES), BF)
        zero = jnp.zeros((nrow, LANES), BF)
        kb = dot(jnp.where(cl == rank + rn, spread, zero), ones)
        kb_ref[...] = kb
        loc["qb"][...] = dot(jnp.where(cl == rank + N + rn, spread, zero), ones)
        keepb = dot(jnp.where(cl == rank + 2 * N, spread, zero), ones)
        loc["k2"][...] = jnp.where(keepb > 0.5, -LOG2E * kb * kb, -1e30)
        keep("qb", layer)
        keep("k2", layer)
        ec = 512
        nt = ec // LANES
        un = 8
        k2_ref, ex_ref, us_ref = loc["k2"], loc["ex"], loc["us"]

        def chunk(ci, carry, layer=layer):
            e0 = pl.multiple_of(ci * ec, ec)

            def body(i, sd):
                s, d = [list(v) for v in sd]
                g0 = pl.multiple_of(i * un, un)
                for t in range(un):
                    r = pl.multiple_of(g0 * N + t * N, N)
                    k2 = k2_ref[pl.ds(r, N), :]
                    kv = kb_ref[pl.ds(r, N), :]
                    for j in range(nt):
                        lane = pl.ds(e0 + LANES * j, LANES)
                        a = jnp.exp2(k2 * ex_ref.at[pl.ds(g0, un), lane][t : t + 1, :])
                        s[j] = a * s[j] + kv * us_ref.at[pl.ds(g0, un), lane][t : t + 1, :]
                        d[j] = a * d[j]
                return tuple(s), tuple(d)

            zeros = tuple(jnp.zeros((N, LANES), F32) for _ in range(nt))
            one = tuple(jnp.ones((N, LANES), F32) for _ in range(nt))
            s, d = lax.fori_loop(0, t_len // un, body, (zeros, one))
            for j in range(nt):
                lane = pl.ds(e0 + LANES * j, LANES)
                c_src[layer, 0:N, lane] = d[j].astype(BF)
                c_src[layer, N : 2 * N, lane] = s[j].astype(BF)
            return carry

        lax.fori_loop(0, inner // ec, chunk, 0)
        cr = Carry(sec, me, n, c_src.at[layer], c_recv.at[layer], c_pre.at[layer], c_dst.at[layer],
                   [s.at[layer] for s in (c1, c2, c3, c4)], None, inner)
        cr.decay_out = loc["dec"]
        carries.append(cr)
        if layer == 1:
            for name in ("dec", "sb", "y"):
                kept(name, 0)
        cr.send()
        ut_s[layer] = u.T.reshape(ut_s.shape[1:])
        cr.combine()
        keep("dec", layer)
        cr.get()
        st[...] = c_dst[layer].astype(F32)
        part_send(0, layer)

        def s_copy(blk, slot, layer=layer):
            return pltpu.make_async_copy(
                sbuf.at[slot], hbm[layer]["s"].at[pl.ds(pl.multiple_of(blk * BT * N, BT * N), BT * N), :], s_sem.at[slot])

        steps = t_len // BT

        def block(i, carry, s_copy=s_copy, vec=vec):
            slot = lax.rem(i, 2)
            rows = pl.ds(pl.multiple_of(i * BT, BT), BT)
            rbase = pl.multiple_of(i * BT * N, BT * N)

            @pl.when(i >= 2)
            def _():
                s_copy(i - 2, slot).wait()

            loc["sb"][rows, :] = st[...].astype(BF)
            qbd = block_diag(loc["proj"][rows, :], rank + N).astype(BF)
            s_ref = sbuf.at[slot]
            for ci in range(inner // ec):
                e0 = ci * ec
                s = [st[:, pl.ds(e0 + LANES * j, LANES)] for j in range(nt)]
                for t in range(BT):
                    krow = pl.ds(pl.multiple_of(rbase + t * N, N), N)
                    k2 = k2_ref[krow, :]
                    kv = kb_ref[krow, :]
                    for j in range(nt):
                        lane = pl.ds(e0 + LANES * j, LANES)
                        a = jnp.exp2(k2 * ex_ref.at[rows, lane][t : t + 1, :])
                        s[j] = a * s[j] + kv * us_ref.at[rows, lane][t : t + 1, :]
                        s_ref[t * N : (t + 1) * N, lane] = s[j].astype(BF)
                for j in range(nt):
                    st[:, pl.ds(e0 + LANES * j, LANES)] = s[j]
                at = pl.ds(e0, ec)
                c = loc["c"][rows, at]
                y = dot(qbd, s_ref[:, at]) + vec[6:7, at] * (c * jax.nn.sigmoid(c))
                loc["y"][rows, at] = y
                z = loc["z"][rows, at]
                o_all[rows, at] = (y * (z * jax.nn.sigmoid(z))).astype(BF)
            s_copy(i, slot).start()
            return carry

        lax.fori_loop(0, steps, block, 0)
        keep("sb", layer)
        keep("y", layer)
        part_forward(0, layer)
        if layer == 0:
            @pl.when(sec == 1)
            def _():
                oth(0).wait_recv()
                out_copy(out_oth).start()

            @pl.when(sec == 0)
            def _():
                oth(1).wait_recv()
                for k in in_order:
                    in_copy(k, in_oth).start()

        out_copy(out_own).wait()
        o = o_all[...]
        hn = (hrow[...].astype(F32) + dot(o, w_out[...])).astype(BF)
        if layer == 0:
            hrow[...] = hn
            hmid_ref[...] = hn
            send_rim(1)

            @pl.when(sec == 0)
            def _():
                oth(0).wait_recv()
                out_copy(out_oth).start()

            @pl.when(sec == 1)
            def _():
                oth(1).wait_recv()
                out_copy(out_own).start()
        else:
            hout_ref[...] = hn
        ot_s[layer] = o.T.reshape(ot_s.shape[1:])
        part_send(1, layer)
        for slot in range(2):
            s_copy(steps - 2 + slot, slot).wait()
        if layer == 0:
            for name in SAVED:
                if name not in ("dec", "sb", "y"):
                    kept(name, 0)

    for name in SAVED:
        kept(name, 1)
    for layer in range(2):
        part_forward(1, layer)
    for layer in range(2):
        for kind in range(2):
            part_own(kind, layer).wait()
            for i in range(2):
                part_arrived(kind, layer, 2 * (1 - sec) + (x if i == 0 else 1 - x))
            for k in range(3):
                part_copy(kind, layer, k, None, None).wait_send()
    for cp in small:
        cp.wait_send()
    for k in range(2):
        oth(k).wait_send()

    @pl.when(sec == 0)
    def _():
        for k in in_order:
            xz_copy(k, t_len if k >= n_half else rim + t_len).wait_send()

    for layer in range(2):
        @pl.when(has_rim(layer, me < n - 1))
        def _(layer=layer):
            rim_copy(layer, me + 1).wait_send()

    for cr in carries:
        cr.sent()


def forward(n, rank, cid, bounds, tokens, smalls, in_own, out_own):
    t_len, width = tokens.shape[1:]
    inner = out_own.shape[0]
    rim = 16
    rows = t_len * N

    def f32(*s):
        return jax.ShapeDtypeStruct(s, F32)

    def b16(*s):
        return jax.ShapeDtypeStruct(s, BF)

    shapes = {
        "xi": f32(t_len + rim, inner), "z": f32(t_len, inner), "c": f32(t_len, inner), "beta": f32(t_len, inner),
        "ex": f32(t_len, inner), "us": f32(t_len, inner), "k2": f32(rows, LANES), "qb": f32(rows, LANES),
        "y": f32(t_len, inner), "proj": b16(t_len, LANES), "dec": b16(n, N, LANES), "sb": b16(t_len, inner),
    }
    outs = [
        b16(width, 2 * inner), b16(inner, width), f32(t_len, LANES), b16(2, inner, LANES), b16(2, LANES, inner),
        f32(2, 8, inner), b16(t_len, width), b16(t_len, width),
    ]
    specs = [ANYSPEC, ANYSPEC] + [VSPEC] * 6
    for _ in range(2):
        outs += [shapes[name] for name in SAVED]
        outs += [b16(rows, inner), b16(n // 2, width // n, 4 * t_len), b16(n // 2, inner // n, 4 * t_len)]
        specs += [ANYSPEC] * (len(SAVED) + 3)
    scratch = [pltpu.VMEM(shapes[name].shape, shapes[name].dtype) for name in SAVED]
    scratch += [
        pltpu.VMEM((rows, LANES), F32), pltpu.VMEM((width, 2 * inner), BF), pltpu.VMEM((inner, width), BF),
        pltpu.VMEM((2 * inner // 512, rim + t_len, 512), F32), pltpu.VMEM((2, 2, rim, width), BF),
        pltpu.VMEM((t_len, width), BF), pltpu.VMEM((N, inner), F32), pltpu.VMEM((2, BT * N, inner), BF),
        pltpu.VMEM((t_len, inner), BF), pltpu.VMEM((2, n // 2, 2, width // n, t_len), BF),
        pltpu.VMEM((2, n // 2, 2, inner // n, t_len), BF),
        pltpu.VMEM((2, 2 * N, inner), BF), pltpu.VMEM((2, n, 2 * N, LANES), BF), pltpu.VMEM((2, n, N, LANES), BF),
        pltpu.VMEM((2, N, inner), BF),
    ]
    dma = pltpu.SemaphoreType.DMA
    n_in = 2 * inner // 512
    scratch += [
        dma((2, len(SAVED))), dma((n_in,)), dma(()), dma((3,)), dma((3,)), dma((n_in,)), dma((n_in,)), dma((2,)), dma((2,)),
        dma((2,)), dma((2,)), dma((2,)), dma((2, 2, 3)), dma((2, 2, 4)), dma((2, 2)),
        dma((2, n)), dma((2, n)), dma((2, n)), dma((2, n)),
    ]
    res = pl.pallas_call(
        functools.partial(forward_kernel, n, rank),
        out_shape=outs,
        in_specs=[pl.BlockSpec(memory_space=pltpu.SMEM)] + [VSPEC] * 8 + [ANYSPEC] * 2,
        out_specs=specs,
        scratch_shapes=scratch,
        compiler_params=pltpu.CompilerParams(vmem_limit_bytes=60 * MIB, collective_id=cid, has_side_effects=True),
        name="forward",
    )(bounds, tokens, *smalls, in_own, out_own)
    first, rest = res[:8], res[8:]
    per = len(SAVED) + 3
    saved = [dict(zip(SAVED + ("s", "ut4", "ot4"), rest[i * per : (i + 1) * per])) for i in range(2)]
    return first, saved


class Sub:
    def __init__(self, kit, num, layer, buf, recvs, out, lane0, lanes, steps, held):
        self.kit, self.num, self.layer = kit, num, layer
        self.at = pl.ds(lane0, lanes)
        self.buf, self.recvs, self.out = buf, recvs, out
        self.steps, self.held = steps, held
        self.last = len(steps) - 1
        self.stage = 0

    def bit(self, what):
        return self.kit.sec if what == "s" else self.kit.mybit[what]

    def partner(self, i):
        kit, what = self.kit, self.steps[i]
        if what == "s":
            return (1 - kit.sec, kit.me)
        return (kit.sec, kit.me + 2**what * (1 - 2 * kit.mybit[what]))

    def index(self, i, away):
        done = {w: self.bit(w) for w in self.steps[:i]}
        what = self.steps[i]
        done[what] = 1 - self.bit(what) if away else self.bit(what)
        return tuple(done.get(w, slice(None)) for w in self.held)

    def copy(self, i):
        free = len(self.held) - 1 - i
        return pltpu.make_async_remote_copy(
            src_ref=self.buf.at[self.index(i, True) + (slice(None), self.at)],
            dst_ref=self.recvs[i].at[(slice(None),) * (free + 1) + (self.at,)],
            send_sem=self.kit.ssem.at[self.layer, self.num, i], recv_sem=self.kit.rsem.at[self.layer, self.num, i],
            device_id=self.partner(i), device_id_type=MESH)

    def begin(self):
        self.copy(0).start()

    def place(self, half):
        return self.kit.place[self.out](half, self.at)

    def final(self):
        kit = self.kit
        return pltpu.make_async_remote_copy(
            src_ref=kit.res[self.out].at[:, self.at], dst_ref=self.place(1 - self.layer),
            send_sem=kit.fsem.at[self.layer, self.num], recv_sem=kit.frsem.at[self.layer, self.num],
            device_id=(1 - kit.sec, kit.me), device_id_type=MESH)

    def advance(self):
        i = self.stage
        if i > self.last:
            return
        kit = self.kit
        self.copy(i).wait_recv()
        free = len(self.held) - 1 - i
        fixed = self.index(i, False)
        res = kit.res[self.out]

        def body(k, carry):
            sub = list(unpack_index(k, free))
            src = tuple(sub) + (slice(None), self.at)
            dst = tuple(sub.pop(0) if isinstance(f, slice) else f for f in fixed) + (slice(None), self.at)
            if i == self.last:
                val = self.buf[dst].astype(F32) + self.recvs[i][src].astype(F32)

                @pl.when(kit.sec == self.layer)
                def _():
                    self.place(self.layer)[...] = val

                @pl.when(kit.sec != self.layer)
                def _():
                    res[:, self.at] = val
            else:
                self.buf[dst] = self.buf[dst] + self.recvs[i][src]
            return carry

        if free:
            lax.fori_loop(0, 2**free, body, 0)
        else:
            body(0, 0)
        self.stage = i + 1
        if i < self.last:
            self.copy(i + 1).start()
        else:
            @pl.when(kit.sec != self.layer)
            def _():
                self.final().start()

    def finish(self):
        assert self.stage > self.last
        for i in range(self.last + 1):
            self.copy(i).wait_send()

        @pl.when(self.kit.sec != self.layer)
        def _():
            self.final().wait_send()

        @pl.when(self.kit.sec == self.layer)
        def _():
            self.final().wait_recv()


class VecSum:
    def __init__(self, kit, layer, acc, send, recv):
        self.kit, self.layer, self.acc, self.send, self.recv = kit, layer, acc, send, recv
        self.stage = 0

    def copy(self, s):
        kit = self.kit
        if s == 0:
            to = (1 - kit.sec, kit.me)
        else:
            to = (kit.sec, kit.me + 2 ** (s - 1) * (1 - 2 * kit.mybit[s - 1]))
        return pltpu.make_async_remote_copy(
            src_ref=self.send.at[self.layer, s], dst_ref=self.recv.at[self.layer, s],
            send_sem=kit.vsem.at[self.layer, s], recv_sem=kit.vrsem.at[self.layer, s],
            device_id=to, device_id_type=MESH)

    def start(self, s):
        self.send[self.layer, s] = self.acc[self.layer].astype(BF)
        self.copy(s).start()

    def begin(self):
        self.start(0)

    def advance(self):
        s = self.stage
        if s > self.kit.bits:
            return
        self.copy(s).wait_recv()
        self.acc[self.layer] = self.send[self.layer, s].astype(F32) + self.recv[self.layer, s].astype(F32)
        self.stage = s + 1
        if s < self.kit.bits:
            self.start(s + 1)

    def drain(self):
        while self.stage <= self.kit.bits:
            self.advance()
        for s in range(self.kit.bits + 1):
            self.copy(s).wait_send()


class Kit:
    pass


class Gather:
    def __init__(self, kit, kind, layer, src, dst):
        self.kit, self.kind, self.layer = kit, kind, layer
        self.src, self.dst = src, dst

    def peers(self):
        kit = self.kit
        x = kit.mybit[0]
        other = kit.me + 1 - 2 * x
        return [(1 - kit.sec, kit.me, x), (kit.sec, other, 1 - x), (1 - kit.sec, other, 1 - x)]

    def copy(self, k, slot):
        kit = self.kit
        sec, dev, bit = self.peers()[k]
        return pltpu.make_async_remote_copy(
            src_ref=self.src(sec, bit), dst_ref=self.dst(slot),
            send_sem=kit.osem.at[self.layer, self.kind, k], recv_sem=kit.orsem.at[self.layer, self.kind, slot],
            device_id=(sec, dev), device_id_type=MESH)

    def slot(self, sec, bit):
        return 2 * sec + bit

    def send(self, order=(1, 2, 0)):
        mine = self.slot(self.kit.sec, self.kit.mybit[0])
        for k in order:
            self.copy(k, mine).start()

    def wait(self):
        for k in range(3):
            sec, dev, bit = self.peers()[k]
            self.copy(k, self.slot(sec, bit)).wait_recv()

    def sent(self):
        mine = self.slot(self.kit.sec, self.kit.mybit[0])
        for k in range(3):
            self.copy(k, mine).wait_send()


LOADS = ("h", "xi", "z", "c", "proj", "beta", "ex", "us", "k2", "qb", "sb", "y", "dec")
BOTH = ("h", "proj", "dec", "sb")
BIG = ("go", "gz", "gx")


def lane_parts(lanes):
    unit = lanes // LANES
    a = max(1, (3 * unit) // 4)
    return [(0, a * LANES), (a * LANES, lanes - a * LANES)]


def bit_orders(bits):
    low = list(range(1, bits))
    return [low, [2, 1] + low[2:]]


def back_kernel(n, rank, shapes, *refs):
    refs = list(refs)

    def take(k):
        out = refs[:k]
        del refs[:k]
        return out

    cots, mask_ref, in_own, in_oth, out_own, out_oth = take(6)
    hbm = [dict(zip(LOADS + ("s", "ut4", "ot4"), take(len(LOADS) + 3))) for _ in range(2)]
    vec2, xp2, dtp2 = take(3)
    dh_out, gin_out, gout_out, gsm_out, vec_out = take(5)
    loc = {name: (take(2) if name in BOTH else take(1) * 2) for name in LOADS}
    (g_both, w_out, w_in, sbuf, qs2, ws2, bst, deps, dkq, dy_ref, dz_both, dx_both, gdt_ref, gtmp, rims, rimr) = take(16)
    dxc = loc["y"][0]
    ut4, ot4, dr4, dz4, dx4 = take(5)
    kit = Kit()
    bits, me, mybit = coords(n)
    bufs = [dict(zip(BIG + ("sm",), take(4))) for _ in range(2)]
    recvs = []
    for _ in range(2):
        got = {name: take(bits - 1) for name in BIG}
        got["sm"] = take(bits + 1)
        recvs.append(got)
    kit.res = dict(zip(BIG + ("sm",), take(4)))
    vacc, vsend, vrecv = take(3)
    c_src, c_recv, c_pre, c_dst = take(4)
    (ld_sem, g_sem, wo_sem, wi_sem, s_sem, rim_sem, rimr_sem, own_sem, kit.osem, kit.orsem, kit.ssem, kit.rsem,
     kit.fsem, kit.frsem, kit.vsem, kit.vrsem, c1, c2, c3, c4) = take(20)
    assert not refs
    sec = lax.axis_index("section")
    kit.sec, kit.me, kit.bits, kit.mybit = sec, me, bits, mybit
    t_len, width = dh_out.shape
    inner = w_out.shape[0]
    cb = 512
    lead = shapes["lead"]

    barrier = pltpu.get_barrier_semaphore()
    for k in range(1, n):
        pl.semaphore_signal(barrier, inc=1, device_id=(sec, lax.rem(me + k, n)), device_id_type=MESH)
    for to in (me, me + 1 - 2 * mybit[0]):
        pl.semaphore_signal(barrier, inc=1, device_id=(1 - sec, to), device_id_type=MESH)

    pos = {name: i for i, name in enumerate(LOADS)}

    def load(name, layer):
        return pltpu.make_async_copy(hbm[layer][name], loc[name][layer], ld_sem.at[pos[name], layer])

    def out_chunk(k, src):
        at = pl.ds(k * cb, cb)
        return src.at[at, :], w_out.at[at, :], wo_sem.at[k]

    def in_chunk(k, slot, src):
        return src.at[:, pl.ds(k * cb, cb)], w_in.at[slot], wi_sem.at[slot]

    def fetch(layer, chunk, own, oth):
        a, b, s = chunk(own)
        a2 = chunk(oth)[0]

        @pl.when(sec == layer)
        def _():
            pltpu.make_async_copy(a, b, s).start()

        @pl.when(sec != layer)
        def _():
            pltpu.make_async_copy(a2, b, s).start()

    def arrive(chunk, own):
        a, b, s = chunk(own)
        pltpu.make_async_copy(a, b, s).wait()

    n_out = inner // cb
    n_in = 2 * inner // cb
    in_order = list(range(n_in // 2, n_in)) + list(range(n_in // 2))
    slots = w_in.shape[0]

    cot_hbm = cots.at[sec]
    pltpu.make_async_copy(cot_hbm, g_both.at[1], g_sem).start()
    for k in range(n_out):
        fetch(1, lambda src, k=k: out_chunk(k, src), out_own, out_oth)
    for name in ("z", "y", "c", "ex", "k2", "qb", "dec", "proj", "beta", "us", "sb", "xi", "h"):
        load(name, 1).start()
    for name in BOTH:
        load(name, 0).start()
    for i in range(slots):
        fetch(1, lambda src, i=i: in_chunk(in_order[i], i, src), in_own, in_oth)

    half_go = width // 2
    half_in = inner // 2
    kit.place = {
        "go": lambda hf, at: gout_out.at[:, pl.ds(hf * half_go + at.start, at.size)],
        "gz": lambda hf, at: gin_out.at[:, pl.ds(inner + hf * half_in + at.start, at.size)],
        "gx": lambda hf, at: gin_out.at[:, pl.ds(hf * half_in + at.start, at.size)],
        "sm": lambda hf, at: gsm_out.at[hf, :, at],
    }
    halves = [2] * (bits - 1)
    subs = []
    for layer in range(2):
        mine = {}
        num = 0
        for name, lanes in (("go", half_go), ("gz", half_in), ("gx", half_in)):
            mine[name] = []
            for (l0, ln), order in zip(lane_parts(lanes), bit_orders(bits)):
                mine[name].append(
                    Sub(kit, num, layer, bufs[layer][name], recvs[layer][name], name, l0, ln, order,
                        list(range(bits - 1, 0, -1))))
                num += 1
        mine["sm"] = [Sub(kit, num, layer, bufs[layer]["sm"], recvs[layer]["sm"], "sm", 0, LANES,
                          ["s", 2, 1, 0] + list(range(3, bits)), ["s"] + list(range(bits - 1, -1, -1)))]
        subs.append(mine)

    def begin(name, layer):
        for s in subs[layer][name]:
            s.begin()

    def advance(layer, *names):
        for name in names:
            for s in subs[layer][name]:
                s.advance()

    rows_go = inner // n
    rows_in = width // n
    rows_sm = inner // n
    x = mybit[0]

    def owner(j, count):
        return tuple((j >> (count - 1 - d)) & 1 for d in range(count))

    my_slot = 2 * sec + x

    def operands(layer):
        half = n // 2

        def lanes_of(ref, size):
            return lambda sc, b: ref.at[:, pl.ds(pl.multiple_of(sc * size, LANES), size)]

        def rows_of(ref):
            return lambda slot: ref.at[layer, slot]

        return {
            "dr": Gather(kit, 0, layer, lanes_of(g_both.at[layer], half_go), rows_of(dr4)),
            "dz": Gather(kit, 1, layer, lanes_of(dz_both.at[layer], half_in), rows_of(dz4)),
            "dx": Gather(kit, 2, layer, lanes_of(dx_both.at[layer], half_in), rows_of(dx4)),
        }

    ops = [operands(layer) for layer in range(2)]

    def part_load(layer, k):
        src, dst = (("ut4", ut4), ("ot4", ot4))[k]
        return pltpu.make_async_copy(hbm[layer][src], dst.at[layer], own_sem.at[layer, k])

    def own_half(ref, layer, size):
        return ref[layer, :, pl.ds(pl.multiple_of(sec * size, LANES), size)]

    pl.semaphore_wait(barrier, n + 1)
    vecs = [VecSum(kit, layer, vacc, vsend, vrecv) for layer in range(2)]
    pltpu.make_async_copy(cot_hbm, g_both.at[1], g_sem).wait()
    ops[1]["dr"].send()
    for layer in (1, 0):
        for k in range(2):
            part_load(layer, k).start()

    def grad_go(layer):
        ops[layer]["dr"].wait()
        part_load(layer, 1).wait()
        dr4[layer, my_slot] = own_half(g_both, layer, half_go)
        rhs = dr4[layer].reshape(4 * t_len, half_go)
        for j in range(n // 2):
            bufs[layer]["go"][owner(j, bits - 1)] = dot(ot4[layer, j], rhs).astype(BF)
        begin("go", layer)

    def grad_in(name, layer, key, both, four):
        ops[layer][key].wait()
        if name == "gz":
            part_load(layer, 0).wait()
        four[layer, my_slot] = own_half(both, layer, half_in)
        lhs = ut4[layer].reshape(n // 2 * rows_in, 4 * t_len)
        step = 512
        for l0 in range(0, half_in, step):
            at = pl.ds(l0, step)
            g = dot(lhs, four[layer, :, :, at].reshape(4 * t_len, step)).astype(BF)
            for j in range(n // 2):
                bufs[layer][name][owner(j, bits - 1) + (slice(None), at)] = g[j * rows_in : (j + 1) * rows_in]
        begin(name, layer)


    carries = []
    for layer in (1, 0):
        g_ref = g_both.at[layer]
        dz_ref = dz_both.at[layer]
        L = {name: loc[name][layer] for name in LOADS}
        vec, xp, dtp = vec2.at[layer], xp2.at[layer], dtp2.at[layer]
        vacc[layer] = jnp.zeros(vacc.shape[1:], F32)
        for name in ("z", "y", "c"):
            load(name, layer).wait()
        dr = g_ref[...]
        for k in range(n_out):
            at = pl.ds(k * cb, cb)
            arrive(lambda src, k=k: out_chunk(k, src), out_own)
            do = dot_nt(dr, w_out[at, :])
            act, der = silu_parts(L["z"][:, at])
            dy = do * act
            dy_ref[:, at] = dy
            dz_ref[:, at] = (do * L["y"][:, at] * der).astype(BF)
            c = L["c"][:, at]
            vacc[layer, 6:7, at] = jnp.sum(dy * (c * jax.nn.sigmoid(c)), axis=0, keepdims=True)
        if layer == 1:
            for k in range(n_out):
                fetch(0, lambda src, k=k: out_chunk(k, src), out_own, out_oth)
            load("z", 0).start()
        for name in ("ex", "k2", "qb"):
            load(name, layer).wait()
        k2_ref, qb_ref, ex_ref = L["k2"], L["qb"], L["ex"]
        ec = 512
        nt = ec // LANES
        un = 8

        def chunk(ci, carry, k2_ref=k2_ref, qb_ref=qb_ref, ex_ref=ex_ref, layer=layer):
            e0 = pl.multiple_of(ci * ec, ec)

            def body(i, b):
                b = list(b)
                g0 = pl.multiple_of((t_len // un - 1 - i) * un, un)
                for t in range(un - 1, -1, -1):
                    r = pl.multiple_of(g0 * N + t * N, N)
                    k2 = k2_ref[pl.ds(r, N), :]
                    qv = qb_ref[pl.ds(r, N), :]
                    for j in range(nt):
                        lane = pl.ds(e0 + LANES * j, LANES)
                        a = jnp.exp2(k2 * ex_ref.at[pl.ds(g0, un), lane][t : t + 1, :])
                        b[j] = a * (qv * dy_ref.at[pl.ds(g0, un), lane][t : t + 1, :] + b[j])
                return tuple(b)

            b = lax.fori_loop(0, t_len // un, body, tuple(jnp.zeros((N, LANES), F32) for _ in range(nt)))
            for j in range(nt):
                c_src[layer, :, pl.ds(e0 + LANES * j, LANES)] = b[j].astype(BF)
            return carry

        lax.fori_loop(0, inner // ec, chunk, 0)
        load("dec", layer).wait()
        cr = Carry(sec, me, n, c_src.at[layer], c_recv.at[layer], c_pre.at[layer], c_dst.at[layer],
                   [s.at[layer] for s in (c1, c2, c3, c4)], L["dec"], inner)
        carries.append(cr)
        cr.send()
        if layer == 0:
            advance(1, "sm")
            vecs[1].advance()
        cr.combine()
        steps = t_len // BT

        def s_copy(blk, slot, layer=layer):
            return pltpu.make_async_copy(
                hbm[layer]["s"].at[pl.ds(pl.multiple_of(blk * BT * N, BT * N), BT * N), :], sbuf.at[slot],
                s_sem.at[slot])

        s_copy(steps - 1, 0).start()
        for name in ("proj", "beta", "us", "sb"):
            load(name, layer).wait()
        cr.get()
        bst[...] = c_dst[layer].astype(F32)
        ops[layer]["dz"].send()
        if layer == 0:
            grad_in("gx", 1, "dx", dx_both, dx4)

        def block(i, carry, L=L, vec=vec, s_copy=s_copy, dy_ref=dy_ref):
            blk = steps - 1 - i
            slot = lax.rem(i, 2)
            base = pl.multiple_of(blk * BT, BT)
            rows = pl.ds(base, BT)
            rbase = pl.multiple_of(blk * BT * N, BT * N)

            @pl.when(i + 1 < steps)
            def _():
                s_copy(blk - 1, 1 - slot).start()

            s_copy(blk, slot).wait()
            projb = L["proj"][rows, :]
            pf = projb.astype(F32)
            cols = iota((BT, LANES), 1)
            is_k = (cols >= rank) & (cols < rank + N)
            ksum = jnp.sum(jnp.where(is_k, pf * pf, 0.0), axis=-1, keepdims=True)
            kbd = block_diag(projb, rank)
            k2bd = (kbd * kbd).astype(BF)
            kbd = kbd.astype(BF)
            r1 = jnp.zeros((BT, BT * N), F32)
            r2 = jnp.zeros((BT, BT * N), F32)
            r3 = jnp.zeros((BT, BT * N), F32)
            s_blk = sbuf.at[slot]
            for ci in range(inner // ec):
                e0 = ci * ec
                qs, ws = qs2.at[ci % 2], ws2.at[ci % 2]
                b = [bst[:, pl.ds(e0 + LANES * j, LANES)] for j in range(nt)]
                for t in range(BT - 1, -1, -1):
                    row = slice(t * N, (t + 1) * N)
                    krow = pl.ds(pl.multiple_of(rbase + t * N, N), N)
                    k2 = L["k2"][krow, :]
                    qv = L["qb"][krow, :]
                    for j in range(nt):
                        lane = pl.ds(e0 + LANES * j, LANES)
                        a = jnp.exp2(k2 * L["ex"].at[rows, lane][t : t + 1, :])
                        q = qv * dy_ref.at[rows, lane][t : t + 1, :] + b[j]
                        b[j] = a * q
                        prev = s_blk[(t - 1) * N : t * N, lane] if t > 0 else L["sb"][rows, lane]
                        qs[row, LANES * j : LANES * (j + 1)] = q.astype(BF)
                        ws[row, LANES * j : LANES * (j + 1)] = (b[j] * prev.astype(F32)).astype(BF)
                for j in range(nt):
                    bst[:, pl.ds(e0 + LANES * j, LANES)] = b[j]
                at = pl.ds(e0, ec)
                p1 = dot(kbd, qs[...])
                p2 = dot(k2bd, ws[...])
                c = L["c"][rows, at]
                beta = L["beta"][rows, at]
                eps = beta / (1.0 + beta * ksum)
                dy = dy_ref[rows, at]
                deps[rows, at] = (c * jax.nn.sigmoid(c)) * p1 - p2
                dxc[rows, at] = dy * vec[6:7, at] + eps * p1
                r1 = r1 + dot_nt(L["us"][rows, at].astype(BF), qs[...])
                r2 = r2 + dot_nt(eps.astype(BF), ws[...])
                r3 = r3 + dot_nt(dy.astype(BF), s_blk[:, at])
            same = iota((BT, BT * N), 0) == iota((BT, BT * N), 1) // N
            gather_k = (iota((BT * N, LANES), 1) == rank + iota((BT * N, LANES), 0) % N).astype(F32)
            gather_q = (iota((BT * N, LANES), 1) == rank + N + iota((BT * N, LANES), 0) % N).astype(F32)

            def pick(r, g):
                return jnp.dot(
                    jnp.where(same, r, 0.0), g, precision=lax.Precision.HIGHEST, preferred_element_type=F32)

            dkq[rows, :] = pick(r1, gather_k) - 2.0 * pf * pick(r2, gather_k) + pick(r3, gather_q)
            return carry

        def tick(k, layer=layer):
            if layer == 0:
                advance(1, "sm")
                vecs[1].advance()
            if k == 1:
                if layer == 0:
                    advance(1, "gx")
                grad_go(layer)
                grad_in("gz", layer, "dz", dz_both, dz4)
            if k == 3:
                if layer == 0:
                    advance(1, "gx")
                advance(layer, "go", "gz")

        def block_and_tick(i, carry):
            block(i, carry)
            for k in range(4):
                @pl.when(i == (k + 1) * steps // 4 - 1)
                def _(k=k):
                    tick(k)

            return carry

        lax.fori_loop(0, steps, block_and_tick, 0)
        if layer == 1:
            for name in ("k2", "qb", "ex", "us"):
                load(name, 0).start()
        load("xi", layer).wait()
        projw = L["proj"][...]
        pw = projw.astype(F32)
        colw = iota((t_len, LANES), 1)
        kall = jnp.where((colw >= rank) & (colw < rank + N), pw, 0.0)
        ks = jnp.sum(kall * kall, axis=-1, keepdims=True)
        tc = 256
        def first(k, carry, L=L, dtp=dtp, layer=layer, projw=projw, ks=ks):
            dkc, ddt = carry
            at = pl.ds(pl.multiple_of(k * tc, tc), tc)
            beta = L["beta"][:, at]
            inv = 1.0 / (1.0 + beta * ks)
            dq = deps[:, at] * (inv * inv)
            dkc = dkc + jnp.sum(dq * beta * beta, axis=-1, keepdims=True)
            dp = (dq * beta * (1.0 - beta)).astype(BF)
            vacc[layer, 5:6, at] = jnp.sum(dp.astype(F32), axis=0, keepdims=True)
            gdt_ref[:, at] = dot_tn(projw, dp)[:rank]
            ddt = ddt + dot_nt(dp, dtp[:, at])
            return dkc, ddt

        dkc, ddt = lax.fori_loop(
            0, inner // tc, first, (jnp.zeros((t_len, 1), F32), jnp.zeros((t_len, LANES), F32)))
        dproj = (jnp.where(colw < rank, ddt, dkq[...]) - 2.0 * kall * dkc).astype(BF)
        mask = mask_ref[...]

        def second(k, carry, L=L, xp=xp, layer=layer, dproj=dproj, ck_ref=vec):
            at = pl.ds(pl.multiple_of(k * tc, tc), tc)
            c = L["c"][:, at]
            act, der = silu_parts(c)
            gxp = dot_tn(act.astype(BF), dproj).astype(BF)
            for i in range(tc // rows_sm):
                j = k * (tc // rows_sm) + i
                bufs[layer]["sm"][(0,) + unpack_index(j, bits)] = gxp[i * rows_sm : (i + 1) * rows_sm]
            dc = (dxc[:, at] + dot_nt(dproj, xp[at, :])) * der
            vacc[layer, 4:5, at] = jnp.sum(dc, axis=0, keepdims=True)
            xi = L["xi"][:, at]
            pad = jnp.zeros((8, tc), F32)
            dxi = ck_ref[3:4, at] * dc
            rim = jnp.zeros((8, tc), F32)
            vacc[layer, 3:4, at] = jnp.sum(dc * xi[lead:], axis=0, keepdims=True)
            for j in range(3):
                m = dc * mask[:, j : j + 1]
                vacc[layer, j : j + 1, at] = jnp.sum(m * xi[lead - 3 + j : lead - 3 + j + t_len], axis=0, keepdims=True)
                m = m * ck_ref[j : j + 1, at]
                ext = jnp.concatenate([pad, m, pad], axis=0)
                dxi = dxi + ext[8 + 3 - j : 8 + 3 - j + t_len]
                rim = rim + ext[8 - j : 16 - j]
            deps[:, at] = dxi
            rims[layer, :, at] = jnp.where(iota((8, tc), 0) < 3, rim, 0.0)
            return carry

        lax.fori_loop(0, inner // tc, second, 0)

        def rim_copy(to, layer=layer):
            return pltpu.make_async_remote_copy(
                src_ref=rims.at[layer], dst_ref=rimr.at[layer], send_sem=rim_sem.at[layer], recv_sem=rimr_sem.at[layer],
                device_id=(sec, to), device_id_type=MESH)

        @pl.when(me > 0)
        def _():
            rim_copy(me - 1).start()

        @pl.when(me == n - 1)
        def _():
            rimr[layer] = jnp.zeros(rimr.shape[1:], F32)

        if layer == 1:
            for name in ("c", "beta", "xi", "y"):
                load(name, 0).start()
        prow = rank // n
        for j in range(n):
            for t in range(inner // LANES):
                gtmp[j, t * prow : (t + 1) * prow, :] = gdt_ref[j * prow : (j + 1) * prow, t * LANES : (t + 1) * LANES]
        drow = prow * (inner // LANES)
        for j in range(n):
            bufs[layer]["sm"][(1,) + owner(j, bits) + (slice(0, drow),)] = gtmp[j, 0:drow].astype(BF)
        begin("sm", layer)
        advance(layer, "go", "gz")
        if layer == 0:
            advance(1, "gx")
        du = jnp.zeros((t_len, width), F32)

        def project(du, i, g, layer=layer):
            slot = i % slots
            arrive(lambda src: in_chunk(in_order[i], slot, src), in_own)
            du = du + dot_nt(g, w_in[slot])
            if i + slots < n_in:
                fetch(layer, lambda src: in_chunk(in_order[i + slots], slot, src), in_own, in_oth)
            elif layer == 1:
                fetch(0, lambda src: in_chunk(in_order[i + slots - n_in], slot, src), in_own, in_oth)
            return du

        for i in range(n_in // 2):
            du = project(du, i, dz_ref[:, pl.ds(i * cb, cb)])

        @pl.when(me < n - 1)
        def _():
            rim_copy(me).wait_recv()

        tail = jnp.concatenate([jnp.zeros((5, inner), F32), rimr[layer][0:3]], axis=0)
        deps[pl.ds(t_len - 8, 8), :] = deps[pl.ds(t_len - 8, 8), :] + tail
        dx_both[layer] = deps[...].astype(BF)
        ops[layer]["dx"].send()
        advance(layer, "go", "gz", "sm")
        for i in range(n_in // 2, n_in):
            du = project(du, i, dx_both[layer, :, pl.ds((i - n_in // 2) * cb, cb)])
        load("h", layer).wait()
        hf = L["h"][...].astype(F32)
        inv = lax.rsqrt(jnp.mean(hf * hf, axis=-1, keepdims=True) + NORM_EPS)
        unit = hf * inv
        vacc[layer, 7:8, pl.ds(0, width)] = jnp.sum(du * unit, axis=0, keepdims=True)
        dn = du * vec[7:8, 0:width]
        dh = g_ref[...].astype(F32) + inv * (dn - unit * jnp.mean(dn * unit, axis=-1, keepdims=True))
        if layer == 1:
            g_both[0] = dh.astype(BF)
            ops[0]["dr"].send()
        else:
            dh_out[...] = dh.astype(BF)
        vecs[layer].begin()
        if layer == 0:
            advance(0, "sm")

    grad_in("gx", 0, "dx", dx_both, dx4)
    left = [s for layer in range(2) for v in subs[layer].values() for s in v]
    while any(s.stage <= s.last for s in left) or vecs[0].stage <= bits or vecs[1].stage <= bits:
        for v in vecs[::-1]:
            v.advance()
        for s in left[::-1]:
            s.advance()
    for v in vecs:
        v.drain()
    for layer in range(2):
        vec_out[layer] = vacc[layer]
    for s in left:
        s.finish()
    for layer in range(2):
        for g in ops[layer].values():
            g.sent()

    @pl.when(me > 0)
    def _():
        for layer in range(2):
            pltpu.make_async_remote_copy(
                src_ref=rims.at[layer], dst_ref=rimr.at[layer], send_sem=rim_sem.at[layer], recv_sem=rimr_sem.at[layer],
                device_id=(sec, me - 1), device_id_type=MESH).wait_send()

    for cr in carries:
        cr.sent()


def backward(n, rank, cid, cot, mask, in_own, in_oth, out_own, out_oth, saved, vec2, xp2, dtp2):
    t_len, width = cot.shape[1:]
    inner = out_own.shape[0]
    bits = n.bit_length() - 1
    lead = saved[0]["xi"].shape[0] - t_len
    args = [cot, mask, in_own, in_oth, out_own, out_oth]
    specs = [ANYSPEC, VSPEC] + [ANYSPEC] * 4
    for layer in range(2):
        args += [saved[layer][name] for name in LOADS + ("s", "ut4", "ot4")]
        specs += [ANYSPEC] * (len(LOADS) + 3)
    args += [vec2, xp2, dtp2]
    specs += [VSPEC] * 3
    rows_go, rows_in, rows_sm = inner // n, width // n, inner // n

    def sd(t, *s):
        return jax.ShapeDtypeStruct(s, t)

    outs = [
        sd(BF, t_len, width), sd(F32, rows_in, 2 * inner), sd(F32, rows_go, width), sd(F32, 2, rows_sm, LANES),
        sd(F32, 2, 16, inner),
    ]
    scratch = []
    for name in LOADS:
        a = saved[0][name]
        scratch += [pltpu.VMEM(a.shape, a.dtype)] * (2 if name in BOTH else 1)
    slots = 4
    scratch += [
        pltpu.VMEM((2, t_len, width), BF), pltpu.VMEM((inner, width), BF), pltpu.VMEM((slots, width, 512), BF),
        pltpu.VMEM((2, BT * N, inner), BF), pltpu.VMEM((2, BT * N, 512), BF), pltpu.VMEM((2, BT * N, 512), BF),
        pltpu.VMEM((N, inner), F32), pltpu.VMEM((t_len, inner), F32),
        pltpu.VMEM((t_len, LANES), F32), pltpu.VMEM((t_len, inner), F32), pltpu.VMEM((2, t_len, inner), BF),
        pltpu.VMEM((2, t_len, inner), BF),
        pltpu.VMEM((rank, inner), F32), pltpu.VMEM((n, max(8, rank * inner // (LANES * n)), LANES), F32),
        pltpu.VMEM((2, 8, inner), F32), pltpu.VMEM((2, 8, inner), F32),
    ]
    scratch += [
        pltpu.VMEM((2, n // 2, rows_in, 4 * t_len), BF), pltpu.VMEM((2, n // 2, rows_go, 4 * t_len), BF),
        pltpu.VMEM((2, 4, t_len, width // 2), BF), pltpu.VMEM((2, 4, t_len, inner // 2), BF),
        pltpu.VMEM((2, 4, t_len, inner // 2), BF),
    ]
    dims = (("go", rows_go, width // 2), ("gz", rows_in, inner // 2), ("gx", rows_in, inner // 2), ("sm", rows_sm, LANES))
    for _ in range(2):
        for name, r, ln in dims:
            count = bits + 1 if name == "sm" else bits - 1
            scratch.append(pltpu.VMEM((2,) * count + (r, ln), BF))
    for _ in range(2):
        for name, r, ln in dims:
            count = bits + 1 if name == "sm" else bits - 1
            scratch += [pltpu.VMEM((2,) * (count - 1 - q) + (r, ln), BF) for q in range(count)]
    scratch += [pltpu.VMEM((r, ln), F32) for _, r, ln in dims]
    scratch += [pltpu.VMEM((2, 16, inner), F32)] + [pltpu.VMEM((2, bits + 1, 16, inner), BF)] * 2
    scratch += [
        pltpu.VMEM((2, N, inner), BF), pltpu.VMEM((2, n, N, LANES), BF), pltpu.VMEM((2, n, N, LANES), BF),
        pltpu.VMEM((2, N, inner), BF),
    ]
    nsub = 1 + sum(len(lane_parts(ln)) for _, _, ln in dims[:3])
    dma = pltpu.SemaphoreType.DMA
    scratch += [
        dma((len(LOADS), 2)), dma(()), dma((inner // 512,)), dma((slots,)), dma((2,)), dma((2,)), dma((2,)), dma((2, 2)),
        dma((2, 3, 3)), dma((2, 3, 4)), dma((2, nsub, bits + 1)), dma((2, nsub, bits + 1)),
        dma((2, nsub)), dma((2, nsub)), dma((2, bits + 1)), dma((2, bits + 1)),
        dma((2, n)), dma((2, n)), dma((2, n)), dma((2, n)),
    ]
    return pl.pallas_call(
        functools.partial(back_kernel, n, rank, {"lead": lead}),
        out_shape=outs,
        in_specs=specs,
        out_specs=[VSPEC] * len(outs),
        scratch_shapes=scratch,
        compiler_params=pltpu.CompilerParams(
            vmem_limit_bytes=63 * MIB, collective_id=cid, has_side_effects=True),
        name="backward",
    )(*args)


def on_device(
    tokens, cotangent, bounds, norm_gain, in_proj, conv_kernel, conv_bias, x_proj, dt_proj, dt_bias, skip_gain, out_proj
):
    sec = lax.axis_index("section")
    n = lax.axis_size("ctx")
    me = lax.axis_index("ctx")
    rank = dt_proj.shape[1]
    inner = out_proj.shape[1]
    used = x_proj.shape[2]
    in_own, out_own = in_proj[0], out_proj[0]
    smalls = (norm_gain, conv_kernel[0], conv_bias, dt_bias, skip_gain, x_proj[0], dt_proj[0])
    first, saved = forward(n, rank, 1, bounds, tokens, smalls, in_own, out_own)
    in_oth, out_oth, mask, xp2, dtp2, vec2, hmid, hout = first
    saved[0]["h"] = lax.dynamic_index_in_dim(tokens, sec, 0, keepdims=False)
    saved[1]["h"] = hmid
    dh, g_in, g_out, g_sm, g_vec = backward(
        n, rank, 2, cotangent, mask, in_own, in_oth, out_own, out_oth, saved, vec2, xp2, dtp2)
    vec = lax.dynamic_index_in_dim(g_vec, sec, 0, keepdims=False)

    def share(rows, length):
        size = length // n
        return lax.dynamic_slice_in_dim(vec[rows, :length], me * size, size, axis=1)

    every = share(slice(0, 7), inner)
    tiles = inner // LANES
    prow = rank // n
    g_dt = g_sm[1, : prow * tiles].reshape(tiles, prow, LANES).transpose(1, 0, 2).reshape(prow, inner)
    return (
        hout[None],
        dh[None],
        share(slice(7, 8), tokens.shape[2]),
        g_in[None],
        every[None, 0:4],
        every[4:5],
        g_sm[0][None, :, :used],
        g_dt[None],
        every[5:6],
        every[6:7],
        g_out[None],
    )


def solution(mesh):
    placed = (
        P(None, "ctx", None), P(None, "ctx", None), P(), P("section", None), P("section", None, None),
        P("section", None, None), P("section", None), P("section", None, None), P("section", None, None),
        P("section", None), P("section", None), P("section", None, None),
    )
    return jax.shard_map(
        on_device,
        mesh=mesh,
        in_specs=placed,
        out_specs=(
            P("section", "ctx", None), P("section", "ctx", None), P("section", "ctx"), P("section", "ctx", None),
            P("section", None, "ctx"), P("section", "ctx"), P("section", "ctx", None), P("section", "ctx", None),
            P("section", "ctx"), P("section", "ctx"), P("section", "ctx", None),
        ),
        check_vma=False,
    )
```

profile of v0, /device:TPU:0, one launch (start us, length us, event | category | flops | bytes accessed | tf_op | source)
XLA Modules:
  0.0 263.6 jit_solution(18361262359792312477)
XLA Ops:
  0.6 0.0 copy-start
  0.7 2.1 copy.23
  2.7 76.9 %forward.1 = (bf16[1024,4096]{1,0:T(8,128)(2,1)}, bf16[2048,1024]{1,0:T(8,128)(2,1)}, f32[128,128]{1,0:T(8,128)}, bf16[2,2048,128]{2,1,0:T(8,128)(2,1)}, bf16[2,...) custom-call(s32[2,8]{1,0:T(2,128)} %refs_0_.2, ...), custom_call_target="tpu_custom_call" | custom-call | tf_op jit(solution)/shard_map/forward/pallas_call | solution.py:619
  79.6 0.0 copy-done
  79.6 0.7 dynamic-slice_bitcast_fusion.refs_6_
  80.3 0.0 copy-start.1
  80.3 170.4 %backward.1 = (bf16[128,1024]{1,0:T(8,128)(2,1)}, f32[64,4096]{1,0:T(8,128)}, f32[128,1024]{1,0:T(8,128)}, f32[2,128,128]{2,1,0:T(8,128)}, f32[2,16,2048]{2,1,0:T(8,128)}) custom-call(bf16[2,128,1024]{2,1,0:T(8,128)(2,1)} %refs_0_.3, f32[128,128]{1,0:T(8,128)} %get-tuple-element.55.refs_1_, bf16[1024,4096]{1,0:T(8,128)(2,1)} %bitcast.29, ...), custom_call_target="tpu_custom_call" | custom-call | tf_op jit(solution)/shard_map/backward/pallas_call | solution.py:1401
  250.8 0.9 dynamic-slice_bitcast_fusion.1
  251.7 0.6 constant_dynamic-slice_fusion.1
  252.3 0.7 constant_dynamic-slice_fusion
  253.0 0.6 slice.40
  253.6 0.5 slice_bitcast_fusion.2
  254.1 0.8 slice_bitcast_fusion.1
  254.9 0.7 copy.25
  255.6 1.4 slice.45
  257.0 0.0 copy-done.1
  257.0 0.7 copy.30
  257.7 1.7 copy.31
  259.4 2.3 copy.32
  261.7 1.9 copy.33
  (2 shorter events, 0.0 us)
Async XLA Ops:
  0.6 79.0 %copy-start = (bf16[2,128,1024]{2,1,0:T(8,128)(2,1)S(1)}, bf16[2,128,1024]{2,1,0:T(8,128)(2,1)}, u32[]{:S(2)}) copy-start(bf16[2,128,1024]{2,1,0:T(8,128)(2,1)} %refs_1_.1) | copy-start | bytes 1572868
  80.3 176.7 %copy-start.1 = (bf16[128,1024]{1,0:T(8,128)(2,1)S(1)}, bf16[128,1024]{1,0:T(8,128)(2,1)}, u32[]{:S(2)}) copy-start(bf16[128,1024]{1,0:T(8,128)(2,1)} %get-tuple-element.54) | copy-start | bytes 786436
where the time goes:
time: 264 us
  Pallas kernels  247 us (94%)
  local copies, waits for them, and re-layouts  15.5 us (6%)
    pallas_call x1, Pallas kernels, backward(): pl.pallas_call(functools.partial(back_kernel, n, rank, {'lead': lead}), o...  170 us
    pallas_call x1, Pallas kernels, forward(): pl.pallas_call(functools.partial(forward_kernel, n, rank), out_shape=outs...  76.9 us
    unnamed x10, local copies, waits for them, and re-layouts  9.3 us

commit v1 on v0

--- a/solution.py
+++ b/solution.py
@@ -170,7 +170,7 @@
     neigh = me + 1 - 2 * x
     t_len, width = hout_ref.shape
     inner = w_out.shape[0]
-    used = xproj_ref.shape[1]
+    used = xproj_ref.shape[0]
     cb = 512
     n_half = inner // cb
     rim = rim_ref.shape[2]
@@ -205,7 +205,8 @@
     vec2[sec, 6:7, :] = skip_ref[...].astype(F32)
     vec2[sec, 7:8, 0:width] = gain_ref[...].astype(F32)
     vec2[sec, 7:8, width:inner] = jnp.zeros((1, inner - width), F32)
-    xp2[sec, :, :] = jnp.concatenate([xproj_ref[...], jnp.zeros((inner, LANES - used), BF)], axis=1)
+    xp2[sec, 0:used, :] = xproj_ref[...]
+    xp2[sec, used:LANES, :] = jnp.zeros((LANES - used, inner), BF)
     dtp2[sec, 0:rank, :] = dtproj_ref[...]
     dtp2[sec, rank:LANES, :] = jnp.zeros((LANES - rank, inner), BF)
     row = me * t_len + iota((t_len, LANES), 0)
@@ -255,17 +256,21 @@
         def _():
             rim_copy(layer, me).wait_recv()
 
+    def oth(k):
+        if k == 0:
+            return sibling(out_own, out_oth, oth_s.at[0], oth_r.at[0])
+        return sibling(in_own, in_oth, oth_s.at[1], oth_r.at[1])
+
     send_rim(0)
+
+    @pl.when(sec == 1)
+    def _():
+        oth(1).start()
 
     def xz_copy(k, rows):
         at = pl.ds((k % n_half) * cb, cb)
         dst = loc["z"] if k >= n_half else loc["xi"]
         return sibling(stage.at[k, pl.ds(0, rows), :], dst.at[:, at], xz_s.at[k], xz_r.at[k])
-
-    def oth(k):
-        if k == 0:
-            return sibling(out_own, out_oth, oth_s.at[0], oth_r.at[0])
-        return sibling(in_own, in_oth, oth_s.at[1], oth_r.at[1])
 
     def normed(h, layer):
         hf = h.astype(F32)
@@ -300,8 +305,9 @@
         for k in in_order:
             xz_copy(k, t_len if k >= n_half else rim + t_len).wait_recv()
 
-    oth(0).start()
-    oth(1).start()
+    @pl.when(sec == 0)
+    def _():
+        oth(0).start()
 
     carries = []
     saved = []
@@ -314,7 +320,7 @@
     def kept(name, layer):
         pltpu.make_async_copy(loc[name], hbm[layer][name], sv_sem.at[layer, SAVED.index(name)]).wait()
 
-    def part_copy(kind, layer, k, where_from, where_to):
+    def part_copy(kind, layer, k):
         src = (ut_s, ot_s)[kind].at[layer]
         dst = hbm[layer][("ut4", "ot4")[kind]]
 
@@ -346,13 +352,13 @@
             (ut_s, ot_s)[kind].at[layer, :, x], hbm[layer][("ut4", "ot4")[kind]].at[:, :, at], own_sem.at[layer, kind])
 
     def part_send(kind, layer):
-        part_copy(kind, layer, 0, None, None).start()
-        part_copy(kind, layer, 1, None, None).start()
+        part_copy(kind, layer, 0).start()
+        part_copy(kind, layer, 1).start()
         part_own(kind, layer).start()
 
     def part_forward(kind, layer):
         part_arrived(kind, layer, 2 * sec + 1 - x)
-        part_copy(kind, layer, 2, None, None).start()
+        part_copy(kind, layer, 2).start()
 
     mask = mask_ref[...]
     cols = iota((t_len, LANES), 1)
@@ -381,7 +387,7 @@
             loc["c"][:, at] = c
             xc = c * jax.nn.sigmoid(c)
             loc["us"][:, at] = xc
-            proj = proj + dot(xc.astype(BF), xp[at, :])
+            proj = proj + dot_nt(xc.astype(BF), xp[:, at])
         keep("c", layer)
         projb = jnp.where(cols == rank + 2 * N, keepc, proj).astype(BF)
         loc["proj"][...] = projb
@@ -457,6 +463,16 @@
         cr.get()
         st[...] = c_dst[layer].astype(F32)
         part_send(0, layer)
+        if layer == 0:
+            @pl.when(sec == 0)
+            def _():
+                oth(1).start()
+
+            @pl.when(sec == 1)
+            def _():
+                oth(0).start()
+        else:
+            part_forward(1, 0)
 
         def s_copy(blk, slot, layer=layer):
             return pltpu.make_async_copy(
@@ -535,7 +551,11 @@
         else:
             hout_ref[...] = hn
         ot_s[layer] = o.T.reshape(ot_s.shape[1:])
-        part_send(1, layer)
+        if layer == 0:
+            part_send(1, 0)
+        else:
+            last_o = pltpu.make_async_copy(ot_s.at[1], hbm[1]["ot4"], own_sem.at[1, 1])
+            last_o.start()
         for slot in range(2):
             s_copy(steps - 2 + slot, slot).wait()
         if layer == 0:
@@ -545,15 +565,13 @@
 
     for name in SAVED:
         kept(name, 1)
-    for layer in range(2):
-        part_forward(1, layer)
-    for layer in range(2):
-        for kind in range(2):
-            part_own(kind, layer).wait()
-            for i in range(2):
-                part_arrived(kind, layer, 2 * (1 - sec) + (x if i == 0 else 1 - x))
-            for k in range(3):
-                part_copy(kind, layer, k, None, None).wait_send()
+    last_o.wait()
+    for layer, kind in ((0, 0), (0, 1), (1, 0)):
+        part_own(kind, layer).wait()
+        for i in range(2):
+            part_arrived(kind, layer, 2 * (1 - sec) + (x if i == 0 else 1 - x))
+        for k in range(3):
+            part_copy(kind, layer, k).wait_send()
     for cp in small:
         cp.wait_send()
     for k in range(2):
@@ -591,13 +609,14 @@
         "y": f32(t_len, inner), "proj": b16(t_len, LANES), "dec": b16(n, N, LANES), "sb": b16(t_len, inner),
     }
     outs = [
-        b16(width, 2 * inner), b16(inner, width), f32(t_len, LANES), b16(2, inner, LANES), b16(2, LANES, inner),
+        b16(width, 2 * inner), b16(inner, width), f32(t_len, LANES), b16(2, LANES, inner), b16(2, LANES, inner),
         f32(2, 8, inner), b16(t_len, width), b16(t_len, width),
     ]
     specs = [ANYSPEC, ANYSPEC] + [VSPEC] * 6
-    for _ in range(2):
+    for layer in range(2):
         outs += [shapes[name] for name in SAVED]
-        outs += [b16(rows, inner), b16(n // 2, width // n, 4 * t_len), b16(n // 2, inner // n, 4 * t_len)]
+        outs += [b16(rows, inner), b16(n // 2, width // n, 4 * t_len)]
+        outs += [b16(n // 2, 2, inner // n, t_len) if layer else b16(n // 2, inner // n, 4 * t_len)]
         specs += [ANYSPEC] * (len(SAVED) + 3)
     scratch = [pltpu.VMEM(shapes[name].shape, shapes[name].dtype) for name in SAVED]
     scratch += [
@@ -731,43 +750,73 @@
 
 
 class VecSum:
-    def __init__(self, kit, layer, acc, send, recv):
-        self.kit, self.layer, self.acc, self.send, self.recv = kit, layer, acc, send, recv
+    def __init__(self, kit, layer, n, acc, sib, msg, got, out):
+        self.kit, self.layer, self.n = kit, layer, n
+        self.acc, self.sib, self.msg, self.got, self.out = acc, sib, msg, got, out
         self.stage = 0
 
-    def copy(self, s):
+    def across(self):
         kit = self.kit
-        if s == 0:
-            to = (1 - kit.sec, kit.me)
-        else:
-            to = (kit.sec, kit.me + 2 ** (s - 1) * (1 - 2 * kit.mybit[s - 1]))
         return pltpu.make_async_remote_copy(
-            src_ref=self.send.at[self.layer, s], dst_ref=self.recv.at[self.layer, s],
-            send_sem=kit.vsem.at[self.layer, s], recv_sem=kit.vrsem.at[self.layer, s],
-            device_id=to, device_id_type=MESH)
-
-    def start(self, s):
-        self.send[self.layer, s] = self.acc[self.layer].astype(BF)
-        self.copy(s).start()
+            src_ref=self.acc.at[self.layer], dst_ref=self.sib.at[self.layer],
+            send_sem=kit.vsem.at[self.layer], recv_sem=kit.vrsem.at[self.layer],
+            device_id=(1 - kit.sec, kit.me), device_id_type=MESH)
+
+    def copy(self, k, dev, slot):
+        kit = self.kit
+        return pltpu.make_async_remote_copy(
+            src_ref=self.msg.at[dev], dst_ref=self.got.at[slot],
+            send_sem=kit.v2sem.at[self.layer, k], recv_sem=kit.v2rsem.at[self.layer, slot],
+            device_id=(kit.sec, dev), device_id_type=MESH)
 
     def begin(self):
-        self.start(0)
+        @pl.when(self.kit.sec != self.layer)
+        def _():
+            self.across().start()
 
     def advance(self):
-        s = self.stage
-        if s > self.kit.bits:
+        kit, n = self.kit, self.n
+        if self.stage > 1:
             return
-        self.copy(s).wait_recv()
-        self.acc[self.layer] = self.send[self.layer, s].astype(F32) + self.recv[self.layer, s].astype(F32)
-        self.stage = s + 1
-        if s < self.kit.bits:
-            self.start(s + 1)
+        first = self.stage == 0
+        self.stage += 1
+
+        @pl.when(kit.sec == self.layer)
+        def _():
+            if first:
+                self.across().wait_recv()
+                total = self.acc[self.layer] + self.sib[self.layer]
+                inner = total.shape[1]
+                for j in range(n):
+                    l0 = (j * (inner // n)) // LANES * LANES
+                    g0 = (j * (kit.width // n)) // LANES * LANES
+                    self.msg[j, 0:8, :] = total[:, l0 : l0 + LANES]
+                    self.msg[j, 8:16, :] = total[:, g0 : g0 + LANES]
+                for k in range(1, n):
+                    self.copy(k, lax.rem(kit.me + k, n), kit.me).start()
+                self.got[kit.me] = self.msg[kit.me]
+            else:
+                for k in range(1, n):
+                    frm = lax.rem(kit.me + k, n)
+                    self.copy(k, frm, frm).wait_recv()
+                val = self.got[0]
+                for j in range(1, n):
+                    val = val + self.got[j]
+                self.out[...] = val
 
     def drain(self):
-        while self.stage <= self.kit.bits:
+        kit = self.kit
+        while self.stage < 2:
             self.advance()
-        for s in range(self.kit.bits + 1):
-            self.copy(s).wait_send()
+
+        @pl.when(kit.sec != self.layer)
+        def _():
+            self.across().wait_send()
+
+        @pl.when(kit.sec == self.layer)
+        def _():
+            for k in range(1, self.n):
+                self.copy(k, lax.rem(kit.me + k, self.n), kit.me).wait_send()
 
 
 class Kit:
@@ -820,7 +869,11 @@
 def lane_parts(lanes):
     unit = lanes // LANES
     a = max(1, (3 * unit) // 4)
-    return [(0, a * LANES), (a * LANES, lanes - a * LANES)]
+    return [(0, a * LANES, 0), (a * LANES, lanes - a * LANES, 1)]
+
+
+def two_parts(lanes):
+    return [(0, lanes // 2, 0), (lanes // 2, lanes // 4, 0), (3 * lanes // 4, lanes // 4, 1)]
 
 
 def bit_orders(bits):
@@ -836,7 +889,7 @@
         del refs[:k]
         return out
 
-    cots, mask_ref, in_own, in_oth, out_own, out_oth = take(6)
+    tokens, cots, mask_ref, in_own, in_oth, out_own, out_oth = take(7)
     hbm = [dict(zip(LOADS + ("s", "ut4", "ot4"), take(len(LOADS) + 3))) for _ in range(2)]
     vec2, xp2, dtp2 = take(3)
     dh_out, gin_out, gout_out, gsm_out, vec_out = take(5)
@@ -853,10 +906,10 @@
         got["sm"] = take(bits + 1)
         recvs.append(got)
     kit.res = dict(zip(BIG + ("sm",), take(4)))
-    vacc, vsend, vrecv = take(3)
+    vacc, vsib, vmsg, vgot = take(4)
     c_src, c_recv, c_pre, c_dst = take(4)
     (ld_sem, g_sem, wo_sem, wi_sem, s_sem, rim_sem, rimr_sem, own_sem, kit.osem, kit.orsem, kit.ssem, kit.rsem,
-     kit.fsem, kit.frsem, kit.vsem, kit.vrsem, c1, c2, c3, c4) = take(20)
+     kit.fsem, kit.frsem, kit.vsem, kit.vrsem, kit.v2sem, kit.v2rsem, o_sem, o_rsem, c1, c2, c3, c4) = take(24)
     assert not refs
     sec = lax.axis_index("section")
     kit.sec, kit.me, kit.bits, kit.mybit = sec, me, bits, mybit
@@ -874,7 +927,8 @@
     pos = {name: i for i, name in enumerate(LOADS)}
 
     def load(name, layer):
-        return pltpu.make_async_copy(hbm[layer][name], loc[name][layer], ld_sem.at[pos[name], layer])
+        src = tokens.at[sec] if (name, layer) == ("h", 0) else hbm[layer][name]
+        return pltpu.make_async_copy(src, loc[name][layer], ld_sem.at[pos[name], layer])
 
     def out_chunk(k, src):
         at = pl.ds(k * cb, cb)
@@ -923,30 +977,33 @@
         "gx": lambda hf, at: gin_out.at[:, pl.ds(hf * half_in + at.start, at.size)],
         "sm": lambda hf, at: gsm_out.at[hf, :, at],
     }
-    halves = [2] * (bits - 1)
+    gx_parts = two_parts(half_in)
     subs = []
     for layer in range(2):
         mine = {}
         num = 0
-        for name, lanes in (("go", half_go), ("gz", half_in), ("gx", half_in)):
+        for name, parts in (("go", lane_parts(half_go)), ("gz", lane_parts(half_in)), ("gx", gx_parts)):
             mine[name] = []
-            for (l0, ln), order in zip(lane_parts(lanes), bit_orders(bits)):
+            for l0, ln, which in parts:
                 mine[name].append(
-                    Sub(kit, num, layer, bufs[layer][name], recvs[layer][name], name, l0, ln, order,
+                    Sub(kit, num, layer, bufs[layer][name], recvs[layer][name], name, l0, ln, bit_orders(bits)[which],
                         list(range(bits - 1, 0, -1))))
                 num += 1
         mine["sm"] = [Sub(kit, num, layer, bufs[layer]["sm"], recvs[layer]["sm"], "sm", 0, LANES,
                           ["s", 2, 1, 0] + list(range(3, bits)), ["s"] + list(range(bits - 1, -1, -1)))]
         subs.append(mine)
 
-    def begin(name, layer):
+    def begin(layer, name):
         for s in subs[layer][name]:
             s.begin()
 
     def advance(layer, *names):
         for name in names:
-            for s in subs[layer][name]:
-                s.advance()
+            if name == "vec":
+                vecs[layer].advance()
+            else:
+                for s in subs[layer][name]:
+                    s.advance()
 
     rows_go = inner // n
     rows_in = width // n
@@ -967,10 +1024,19 @@
         def rows_of(ref):
             return lambda slot: ref.at[layer, slot]
 
+        quarter = half_in // 2
+
+        def part_of(ref, p):
+            return lambda sc, b: ref.at[:, pl.ds(pl.multiple_of(sc * half_in + p * quarter, LANES), quarter)]
+
+        def part_to(ref, p):
+            return lambda slot: ref.at[layer, slot, :, pl.ds(p * quarter, quarter)]
+
         return {
             "dr": Gather(kit, 0, layer, lanes_of(g_both.at[layer], half_go), rows_of(dr4)),
             "dz": Gather(kit, 1, layer, lanes_of(dz_both.at[layer], half_in), rows_of(dz4)),
-            "dx": Gather(kit, 2, layer, lanes_of(dx_both.at[layer], half_in), rows_of(dx4)),
+            "dx0": Gather(kit, 2, layer, part_of(dx_both.at[layer], 0), part_to(dx4, 0)),
+            "dx1": Gather(kit, 3, layer, part_of(dx_both.at[layer], 1), part_to(dx4, 1)),
         }
 
     ops = [operands(layer) for layer in range(2)]
@@ -983,36 +1049,70 @@
         return ref[layer, :, pl.ds(pl.multiple_of(sec * size, LANES), size)]
 
     pl.semaphore_wait(barrier, n + 1)
-    vecs = [VecSum(kit, layer, vacc, vsend, vrecv) for layer in range(2)]
+    kit.width = width
+    vecs = [VecSum(kit, layer, n, vacc, vsib, vmsg, vgot, vec_out) for layer in range(2)]
     pltpu.make_async_copy(cot_hbm, g_both.at[1], g_sem).wait()
+    def slot_at(i):
+        return pl.ds(pl.multiple_of(i * t_len, LANES), t_len)
+
+    o_hbm = hbm[1]["ot4"]
+    o_own = pltpu.make_async_copy(o_hbm.at[:, x], ot4.at[1, :, :, slot_at(my_slot)], own_sem.at[1, 1])
+
+    def o_copy(k):
+        i = my_slot if k < 2 else 2 * sec + 1 - x
+        dst = ot4.at[1, :, :, slot_at(i)]
+        src = (o_hbm.at[:, 1 - x], o_hbm.at[:, x], dst)[k]
+        return pltpu.make_async_remote_copy(
+            src_ref=src, dst_ref=dst, send_sem=o_sem.at[k], recv_sem=o_rsem.at[i],
+            device_id=(sec, me + 1 - 2 * x) if k == 0 else (1 - sec, me), device_id_type=MESH)
+
+    def o_wait(i):
+        dst = ot4.at[1, :, :, slot_at(i)]
+        pltpu.make_async_remote_copy(
+            src_ref=dst, dst_ref=dst, send_sem=o_sem.at[0], recv_sem=o_rsem.at[i],
+            device_id=(1 - sec, me), device_id_type=MESH).wait_recv()
+
+    o_copy(0).start()
+    o_copy(1).start()
+    o_own.start()
     ops[1]["dr"].send()
-    for layer in (1, 0):
-        for k in range(2):
-            part_load(layer, k).start()
+    for layer, k in ((1, 0), (0, 1), (0, 0)):
+        part_load(layer, k).start()
 
     def grad_go(layer):
         ops[layer]["dr"].wait()
-        part_load(layer, 1).wait()
+        if layer == 1:
+            o_own.wait()
+            o_wait(2 * (1 - sec) + x)
+            o_wait(2 * (1 - sec) + 1 - x)
+        else:
+            part_load(layer, 1).wait()
         dr4[layer, my_slot] = own_half(g_both, layer, half_go)
         rhs = dr4[layer].reshape(4 * t_len, half_go)
         for j in range(n // 2):
             bufs[layer]["go"][owner(j, bits - 1)] = dot(ot4[layer, j], rhs).astype(BF)
-        begin("go", layer)
-
-    def grad_in(name, layer, key, both, four):
-        ops[layer][key].wait()
-        if name == "gz":
-            part_load(layer, 0).wait()
-        four[layer, my_slot] = own_half(both, layer, half_in)
+
+    def grad_in(name, layer, four, l0):
         lhs = ut4[layer].reshape(n // 2 * rows_in, 4 * t_len)
-        step = 512
-        for l0 in range(0, half_in, step):
-            at = pl.ds(l0, step)
-            g = dot(lhs, four[layer, :, :, at].reshape(4 * t_len, step)).astype(BF)
-            for j in range(n // 2):
-                bufs[layer][name][owner(j, bits - 1) + (slice(None), at)] = g[j * rows_in : (j + 1) * rows_in]
-        begin(name, layer)
-
+        at = pl.ds(l0, cb)
+        g = dot(lhs, four[layer, :, :, at].reshape(4 * t_len, cb)).astype(BF)
+        for j in range(n // 2):
+            bufs[layer][name][owner(j, bits - 1) + (slice(None), at)] = g[j * rows_in : (j + 1) * rows_in]
+
+    def grad_gz(layer):
+        ops[layer]["dz"].wait()
+        part_load(layer, 0).wait()
+        dz4[layer, my_slot] = own_half(dz_both, layer, half_in)
+        for l0 in range(0, half_in, cb):
+            grad_in("gz", layer, dz4, l0)
+        begin(layer, "gz")
+
+    def grad_gx(layer, p):
+        if p == 0:
+            dx4[layer, my_slot] = own_half(dx_both, layer, half_in)
+        ops[layer]["dx0" if p == 0 else "dx1"].wait()
+        for l0 in range(p * half_in // 2, (p + 1) * half_in // 2, cb):
+            grad_in("gx", layer, dx4, l0)
 
     carries = []
     for layer in (1, 0):
@@ -1038,6 +1138,8 @@
             for k in range(n_out):
                 fetch(0, lambda src, k=k: out_chunk(k, src), out_own, out_oth)
             load("z", 0).start()
+        if layer == 0:
+            advance(1, "gz", "vec", "sm")
         for name in ("ex", "k2", "qb"):
             load(name, layer).wait()
         k2_ref, qb_ref, ex_ref = L["k2"], L["qb"], L["ex"]
@@ -1072,10 +1174,15 @@
                    [s.at[layer] for s in (c1, c2, c3, c4)], L["dec"], inner)
         carries.append(cr)
         cr.send()
+        if layer == 1:
+            o_wait(2 * sec + 1 - x)
+            o_copy(2).start()
+        else:
+            grad_go(0)
+        cr.combine()
         if layer == 0:
-            advance(1, "sm")
-            vecs[1].advance()
-        cr.combine()
+            grad_gx(1, 0)
+            grad_gx(1, 1)
         steps = t_len // BT
 
         def s_copy(blk, slot, layer=layer):
@@ -1088,9 +1195,13 @@
             load(name, layer).wait()
         cr.get()
         bst[...] = c_dst[layer].astype(F32)
+        if layer == 0:
+            begin(1, "gx")
+            advance(1, "gz", "vec", "sm")
         ops[layer]["dz"].send()
-        if layer == 0:
-            grad_in("gx", 1, "dx", dx_both, dx4)
+        if layer == 1:
+            grad_go(1)
+        begin(layer, "go")
 
         def block(i, carry, L=L, vec=vec, s_copy=s_copy, dy_ref=dy_ref):
             blk = steps - 1 - i
@@ -1159,18 +1270,20 @@
             return carry
 
         def tick(k, layer=layer):
-            if layer == 0:
+            if layer == 1:
+                if k == 2:
+                    grad_gz(1)
+                if k == 3:
+                    advance(1, "go")
+                return
+            if k == 1:
                 advance(1, "sm")
-                vecs[1].advance()
-            if k == 1:
-                if layer == 0:
-                    advance(1, "gx")
-                grad_go(layer)
-                grad_in("gz", layer, "dz", dz_both, dz4)
+            if k == 2:
+                advance(1, "gx")
+                grad_gz(0)
             if k == 3:
-                if layer == 0:
-                    advance(1, "gx")
-                advance(layer, "go", "gz")
+                advance(0, "go")
+                advance(1, "gx", "sm")
 
         def block_and_tick(i, carry):
             block(i, carry)
@@ -1218,7 +1331,7 @@
             for i in range(tc // rows_sm):
                 j = k * (tc // rows_sm) + i
                 bufs[layer]["sm"][(0,) + unpack_index(j, bits)] = gxp[i * rows_sm : (i + 1) * rows_sm]
-            dc = (dxc[:, at] + dot_nt(dproj, xp[at, :])) * der
+            dc = (dxc[:, at] + dot(dproj, xp[:, at])) * der
             vacc[layer, 4:5, at] = jnp.sum(dc, axis=0, keepdims=True)
             xi = L["xi"][:, at]
             pad = jnp.zeros((8, tc), F32)
@@ -1261,10 +1374,11 @@
         drow = prow * (inner // LANES)
         for j in range(n):
             bufs[layer]["sm"][(1,) + owner(j, bits) + (slice(0, drow),)] = gtmp[j, 0:drow].astype(BF)
-        begin("sm", layer)
-        advance(layer, "go", "gz")
+        begin(layer, "sm")
+        advance(layer, "go")
         if layer == 0:
             advance(1, "gx")
+            advance(0, "gz")
         du = jnp.zeros((t_len, width), F32)
 
         def project(du, i, g, layer=layer):
@@ -1287,7 +1401,8 @@
         tail = jnp.concatenate([jnp.zeros((5, inner), F32), rimr[layer][0:3]], axis=0)
         deps[pl.ds(t_len - 8, 8), :] = deps[pl.ds(t_len - 8, 8), :] + tail
         dx_both[layer] = deps[...].astype(BF)
-        ops[layer]["dx"].send()
+        ops[layer]["dx0"].send()
+        ops[layer]["dx1"].send()
         advance(layer, "go", "gz", "sm")
         for i in range(n_in // 2, n_in):
             du = project(du, i, dx_both[layer, :, pl.ds((i - n_in // 2) * cb, cb)])
@@ -1304,20 +1419,29 @@
         else:
             dh_out[...] = dh.astype(BF)
         vecs[layer].begin()
-        if layer == 0:
-            advance(0, "sm")
-
-    grad_in("gx", 0, "dx", dx_both, dx4)
+
+    parts0 = subs[0]["gx"]
+    advance(0, "sm")
+    grad_gx(0, 0)
+    parts0[0].begin()
+    advance(0, "vec")
+    grad_gx(0, 1)
+    parts0[1].begin()
+    parts0[2].begin()
+    advance(0, "gz", "sm")
+    for _ in range(bits - 1):
+        parts0[0].advance()
+        parts0[2].advance()
+        parts0[1].advance()
+        advance(0, "sm", "vec")
     left = [s for layer in range(2) for v in subs[layer].values() for s in v]
-    while any(s.stage <= s.last for s in left) or vecs[0].stage <= bits or vecs[1].stage <= bits:
-        for v in vecs[::-1]:
-            v.advance()
+    while any(s.stage <= s.last for s in left):
         for s in left[::-1]:
             s.advance()
+    for k in range(3):
+        o_copy(k).wait_send()
     for v in vecs:
         v.drain()
-    for layer in range(2):
-        vec_out[layer] = vacc[layer]
     for s in left:
         s.finish()
     for layer in range(2):
@@ -1335,13 +1459,13 @@
         cr.sent()
 
 
-def backward(n, rank, cid, cot, mask, in_own, in_oth, out_own, out_oth, saved, vec2, xp2, dtp2):
+def backward(n, rank, cid, tokens, cot, mask, in_own, in_oth, out_own, out_oth, saved, vec2, xp2, dtp2):
     t_len, width = cot.shape[1:]
     inner = out_own.shape[0]
     bits = n.bit_length() - 1
     lead = saved[0]["xi"].shape[0] - t_len
-    args = [cot, mask, in_own, in_oth, out_own, out_oth]
-    specs = [ANYSPEC, VSPEC] + [ANYSPEC] * 4
+    args = [tokens, cot, mask, in_own, in_oth, out_own, out_oth]
+    specs = [ANYSPEC, ANYSPEC, VSPEC] + [ANYSPEC] * 4
     for layer in range(2):
         args += [saved[layer][name] for name in LOADS + ("s", "ut4", "ot4")]
         specs += [ANYSPEC] * (len(LOADS) + 3)
@@ -1354,7 +1478,7 @@
 
     outs = [
         sd(BF, t_len, width), sd(F32, rows_in, 2 * inner), sd(F32, rows_go, width), sd(F32, 2, rows_sm, LANES),
-        sd(F32, 2, 16, inner),
+        sd(F32, 16, LANES),
     ]
     scratch = []
     for name in LOADS:
@@ -1385,17 +1509,17 @@
             count = bits + 1 if name == "sm" else bits - 1
             scratch += [pltpu.VMEM((2,) * (count - 1 - q) + (r, ln), BF) for q in range(count)]
     scratch += [pltpu.VMEM((r, ln), F32) for _, r, ln in dims]
-    scratch += [pltpu.VMEM((2, 16, inner), F32)] + [pltpu.VMEM((2, bits + 1, 16, inner), BF)] * 2
+    scratch += [pltpu.VMEM((2, 8, inner), F32)] * 2 + [pltpu.VMEM((n, 16, LANES), F32)] * 2
     scratch += [
         pltpu.VMEM((2, N, inner), BF), pltpu.VMEM((2, n, N, LANES), BF), pltpu.VMEM((2, n, N, LANES), BF),
         pltpu.VMEM((2, N, inner), BF),
     ]
-    nsub = 1 + sum(len(lane_parts(ln)) for _, _, ln in dims[:3])
+    nsub = 1 + 2 + 2 + 3
     dma = pltpu.SemaphoreType.DMA
     scratch += [
         dma((len(LOADS), 2)), dma(()), dma((inner // 512,)), dma((slots,)), dma((2,)), dma((2,)), dma((2,)), dma((2, 2)),
-        dma((2, 3, 3)), dma((2, 3, 4)), dma((2, nsub, bits + 1)), dma((2, nsub, bits + 1)),
-        dma((2, nsub)), dma((2, nsub)), dma((2, bits + 1)), dma((2, bits + 1)),
+        dma((2, 4, 3)), dma((2, 4, 4)), dma((2, nsub, bits + 1)), dma((2, nsub, bits + 1)),
+        dma((2, nsub)), dma((2, nsub)), dma((2,)), dma((2,)), dma((2, n)), dma((2, n)), dma((3,)), dma((4,)),
         dma((2, n)), dma((2, n)), dma((2, n)), dma((2, n)),
     ]
     return pl.pallas_call(
@@ -1410,6 +1534,67 @@
     )(*args)
 
 
+def finish_kernel(n, rank, used, hout, dh, g_in, g_out, g_sm, g_vec, *refs):
+    o_h, o_dh, o_gain, o_in, o_ck, o_cb, o_xp, o_dt, o_dtb, o_skip, o_out, v0, v1, v2, v3, sems = refs
+    moves = ((hout, v0, o_h), (dh, v1, o_dh), (g_in, v2, o_in), (g_out, v3, o_out))
+    loads = [pltpu.make_async_copy(a, v, sems.at[i]) for i, (a, v, _) in enumerate(moves)]
+    stores = [pltpu.make_async_copy(v, b.at[0], sems.at[i]) for i, (_, v, b) in enumerate(moves)]
+    for cp in loads:
+        cp.start()
+    me = lax.axis_index("ctx")
+    inner = o_dt.shape[2]
+    o_xp[0] = g_sm[0].T[0:used]
+    prow = rank // n
+    for t in range(inner // LANES):
+        o_dt[0, :, t * LANES : (t + 1) * LANES] = g_sm[1, t * prow : (t + 1) * prow, :]
+
+    def pick(size, body):
+        for l0 in range(0, LANES, size):
+            @pl.when(lax.rem(me * size, LANES) == l0)
+            def _():
+                body(slice(l0, l0 + size))
+
+    def vectors(at):
+        o_ck[0] = g_vec[0:4, at]
+        o_cb[...] = g_vec[4:5, at]
+        o_dtb[...] = g_vec[5:6, at]
+        o_skip[...] = g_vec[6:7, at]
+
+    def gain(at):
+        o_gain[...] = g_vec[15:16, at]
+
+    pick(o_cb.shape[1], vectors)
+    pick(o_gain.shape[1], gain)
+    for a, b in zip(loads, stores):
+        a.wait()
+        b.start()
+    for cp in stores:
+        cp.wait()
+
+
+def finish(n, rank, used, hout, dh, g_in, g_out, g_sm, g_vec):
+    t_len, width = hout.shape
+    inner = g_in.shape[1] // 2
+    part = inner // n
+
+    def f32(*s):
+        return jax.ShapeDtypeStruct((1,) + s, F32)
+
+    whole = jax.ShapeDtypeStruct((1, t_len, width), BF)
+    return tuple(pl.pallas_call(
+        functools.partial(finish_kernel, n, rank, used),
+        out_shape=[
+            whole, whole, f32(width // n), f32(*g_in.shape), f32(4, part), f32(part), f32(used, part),
+            f32(rank // n, inner), f32(part), f32(part), f32(*g_out.shape),
+        ],
+        in_specs=[ANYSPEC] * 4 + [VSPEC] * 2,
+        out_specs=[ANYSPEC, ANYSPEC, VSPEC, ANYSPEC] + [VSPEC] * 6 + [ANYSPEC],
+        scratch_shapes=[pltpu.VMEM(a.shape, a.dtype) for a in (hout, dh, g_in, g_out)] + [pltpu.SemaphoreType.DMA((4,))],
+        compiler_params=pltpu.CompilerParams(vmem_limit_bytes=60 * MIB),
+        name="finish",
+    )(hout, dh, g_in, g_out, g_sm, g_vec))
+
+
 def on_device(
     tokens, cotangent, bounds, norm_gain, in_proj, conv_kernel, conv_bias, x_proj, dt_proj, dt_bias, skip_gain, out_proj
 ):
@@ -1420,43 +1605,21 @@
     inner = out_proj.shape[1]
     used = x_proj.shape[2]
     in_own, out_own = in_proj[0], out_proj[0]
-    smalls = (norm_gain, conv_kernel[0], conv_bias, dt_bias, skip_gain, x_proj[0], dt_proj[0])
+    smalls = (norm_gain, conv_kernel[0], conv_bias, dt_bias, skip_gain, x_proj[0].T, dt_proj[0])
     first, saved = forward(n, rank, 1, bounds, tokens, smalls, in_own, out_own)
     in_oth, out_oth, mask, xp2, dtp2, vec2, hmid, hout = first
-    saved[0]["h"] = lax.dynamic_index_in_dim(tokens, sec, 0, keepdims=False)
-    saved[1]["h"] = hmid
+    saved[0]["h"] = saved[1]["h"] = hmid
     dh, g_in, g_out, g_sm, g_vec = backward(
-        n, rank, 2, cotangent, mask, in_own, in_oth, out_own, out_oth, saved, vec2, xp2, dtp2)
-    vec = lax.dynamic_index_in_dim(g_vec, sec, 0, keepdims=False)
-
-    def share(rows, length):
-        size = length // n
-        return lax.dynamic_slice_in_dim(vec[rows, :length], me * size, size, axis=1)
-
-    every = share(slice(0, 7), inner)
-    tiles = inner // LANES
-    prow = rank // n
-    g_dt = g_sm[1, : prow * tiles].reshape(tiles, prow, LANES).transpose(1, 0, 2).reshape(prow, inner)
-    return (
-        hout[None],
-        dh[None],
-        share(slice(7, 8), tokens.shape[2]),
-        g_in[None],
-        every[None, 0:4],
-        every[4:5],
-        g_sm[0][None, :, :used],
-        g_dt[None],
-        every[5:6],
-        every[6:7],
-        g_out[None],
-    )
+        n, rank, 2, tokens, cotangent, mask, in_own, in_oth, out_own, out_oth, saved, vec2, xp2, dtp2)
+    outs = finish(n, rank, used, hout, dh, g_in, g_out, g_sm, g_vec)
+    return outs[:6] + (outs[6].transpose(0, 2, 1),) + outs[7:]
 
 
 def solution(mesh):
     placed = (
-        P(None, "ctx", None), P(None, "ctx", None), P(), P("section", None), P("section", None, None),
-        P("section", None, None), P("section", None), P("section", None, None), P("section", None, None),
-        P("section", None), P("section", None), P("section", None, None),
+        P(None, "ctx", None), P(None, "ctx", None), P(), P("section", None), P("section"),
+        P("section"), P("section", None), P("section"), P("section"),
+        P("section", None), P("section", None), P("section"),
     )
     return jax.shard_map(
         on_device,

time: 264 us -> 232 us (0.88)
  Pallas kernels: 247 us -> 229 us
  local copies, waits for them, and re-layouts: 15.5 us -> 0 us
    pallas_call x1, Pallas kernels: 170 us -> 153 us  [backward(): pl.pallas_call(functools.partial(back_kernel, n, rank, {'lead': lead}), o...]
    unnamed x10 -> x0, local copies, waits for them, and re-layouts: 9.3 us -> none
    pallas_call x1, Pallas kernels: 76.9 us -> 72.3 us  [forward(): pl.pallas_call(functools.partial(forward_kernel, n, rank), out_shape=outs...]
    pallas_call x0 -> x1, Pallas kernels: none -> 4.13 us  [finish(): pl.pallas_call(functools.partial(finish_kernel, n, rank, used), out_shape...]
where the time goes in v1:
time: 232 us; the launch traced here: 230 us
  Pallas kernels  229 us (99%)
    pallas_call x1, Pallas kernels, backward(): pl.pallas_call(functools.partial(back_kernel, n, rank, {'lead': lead}), o...  153 us
    pallas_call x1, Pallas kernels, forward(): pl.pallas_call(functools.partial(forward_kernel, n, rank), out_shape=outs...  72.3 us

profile of v1, /device:TPU:0, one launch (start us, length us, event | category | flops | bytes accessed | tf_op | source)
XLA Modules:
  0.0 229.8 jit_solution(9107279135665201383)
XLA Ops:
  0.6 72.3 %forward.1 = (bf16[1024,4096]{1,0:T(8,128)(2,1)}, bf16[2048,1024]{1,0:T(8,128)(2,1)}, f32[128,128]{1,0:T(8,128)}, bf16[2,128,2048]{2,1,0:T(8,128)(2,1)}, bf16[2,...) custom-call(s32[2,8]{1,0:T(2,128)} %refs_0_.2, ...), custom_call_target="tpu_custom_call" | custom-call | tf_op jit(solution)/shard_map/forward/pallas_call | solution.py:638
  73.0 152.5 %backward.1 = (bf16[128,1024]{1,0:T(8,128)(2,1)}, f32[64,4096]{1,0:T(8,128)}, f32[128,1024]{1,0:T(8,128)}, f32[2,128,128]{2,1,0:T(8,128)}, f32[16,128]{1,0:T(8,128)}) custom-call(bf16[2,128,1024]{2,1,0:T(8,128)(2,1)} %refs_0_.3, bf16[2,128,1024]{2,1,0:T(8,128)(2,1)} %refs_1_.3, f32[128,128]{1,0:T(8,128)} %get-tuple-element.66.refs_2_, ...), custom_call_target="tpu_custom_call" | custom-call | tf_op jit(solution)/shard_map/backward/pallas_call | solution.py:1525
  225.5 4.1 %finish.1 = (bf16[1,128,1024]{2,1,0:T(8,128)(2,1)}, bf16[1,128,1024]{2,1,0:T(8,128)(2,1)}, f32[1,64]{1,0:T(1,128)}, f32[1,64,4096]{2,1,0:T(8,128)}, f32[1,4,128]...) custom-call(bf16[128,1024]{1,0:T(8,128)(2,1)} %get-tuple-element.65., ...), custom_call_target="tpu_custom_call" | custom-call | tf_op jit(solution)/shard_map/finish/pallas_call | solution.py:1584

commit v2 on v1

--- a/solution.py
+++ b/solution.py
@@ -873,7 +873,8 @@
 
 
 def two_parts(lanes):
-    return [(0, lanes // 2, 0), (lanes // 2, lanes // 4, 0), (3 * lanes // 4, lanes // 4, 1)]
+    q = lanes // 4
+    return [(0, q, 0), (q, q, 1), (2 * q, q, 0), (3 * q, q, 1)]
 
 
 def bit_orders(bits):
@@ -1138,8 +1139,6 @@
             for k in range(n_out):
                 fetch(0, lambda src, k=k: out_chunk(k, src), out_own, out_oth)
             load("z", 0).start()
-        if layer == 0:
-            advance(1, "gz", "vec", "sm")
         for name in ("ex", "k2", "qb"):
             load(name, layer).wait()
         k2_ref, qb_ref, ex_ref = L["k2"], L["qb"], L["ex"]
@@ -1197,7 +1196,7 @@
         bst[...] = c_dst[layer].astype(F32)
         if layer == 0:
             begin(1, "gx")
-            advance(1, "gz", "vec", "sm")
+            advance(1, "go", "gz", "vec", "sm")
         ops[layer]["dz"].send()
         if layer == 1:
             grad_go(1)
@@ -1273,17 +1272,13 @@
             if layer == 1:
                 if k == 2:
                     grad_gz(1)
-                if k == 3:
-                    advance(1, "go")
                 return
             if k == 1:
                 advance(1, "sm")
             if k == 2:
-                advance(1, "gx")
                 grad_gz(0)
             if k == 3:
-                advance(0, "go")
-                advance(1, "gx", "sm")
+                advance(1, "gz", "gx", "sm", "vec")
 
         def block_and_tick(i, carry):
             block(i, carry)
@@ -1323,47 +1318,75 @@
         dproj = (jnp.where(colw < rank, ddt, dkq[...]) - 2.0 * kall * dkc).astype(BF)
         mask = mask_ref[...]
 
-        def second(k, carry, L=L, xp=xp, layer=layer, dproj=dproj, ck_ref=vec):
+        def rim_copy(to, layer=layer):
+            return pltpu.make_async_remote_copy(
+                src_ref=rims.at[layer], dst_ref=rimr.at[layer], send_sem=rim_sem.at[layer], recv_sem=rimr_sem.at[layer],
+                device_id=(sec, to), device_id_type=MESH)
+
+        for k in range(n_out):
+            at = pl.ds(k * cb, cb)
+            der = silu_parts(L["c"][0:BT, at])[1]
+            dc = (dxc[0:BT, at] + dot(dproj[0:BT], xp[:, at])) * der
+            rim = jnp.zeros((8, cb), F32)
+            for j in range(3):
+                m = dc[0:8] * mask[0:8, j : j + 1] * vec[j : j + 1, at]
+                rim = rim + jnp.concatenate([jnp.zeros((8, cb), F32), m], axis=0)[8 - j : 16 - j]
+            rims[layer, :, at] = jnp.where(iota((8, cb), 0) < 3, rim, 0.0)
+
+        @pl.when(me > 0)
+        def _():
+            rim_copy(me - 1).start()
+
+        @pl.when(me == n - 1)
+        def _():
+            rimr[layer] = jnp.zeros(rimr.shape[1:], F32)
+
+        per_part = half_in // 2 // tc
+
+        def add_rim(p, layer=layer):
+            for hf in range(2):
+                at = pl.ds(hf * half_in + p * half_in // 2, half_in // 2)
+                rows = pl.ds(t_len - BT, BT)
+                edge = jnp.concatenate([jnp.zeros((BT - 3, half_in // 2), F32), rimr[layer, 0:3, at]], axis=0)
+                dx_both[layer, rows, at] = (deps[rows, at] + edge).astype(BF)
+            ops[layer]["dx0" if p == 0 else "dx1"].send()
+
+        def second(i, carry, L=L, xp=xp, layer=layer, dproj=dproj, ck_ref=vec):
+            p, left = i // (2 * per_part), lax.rem(i, 2 * per_part)
+            k = left // per_part * (half_in // tc) + p * per_part + lax.rem(left, per_part)
             at = pl.ds(pl.multiple_of(k * tc, tc), tc)
             c = L["c"][:, at]
             act, der = silu_parts(c)
             gxp = dot_tn(act.astype(BF), dproj).astype(BF)
-            for i in range(tc // rows_sm):
-                j = k * (tc // rows_sm) + i
-                bufs[layer]["sm"][(0,) + unpack_index(j, bits)] = gxp[i * rows_sm : (i + 1) * rows_sm]
+            for r in range(tc // rows_sm):
+                j = k * (tc // rows_sm) + r
+                bufs[layer]["sm"][(0,) + unpack_index(j, bits)] = gxp[r * rows_sm : (r + 1) * rows_sm]
             dc = (dxc[:, at] + dot(dproj, xp[:, at])) * der
             vacc[layer, 4:5, at] = jnp.sum(dc, axis=0, keepdims=True)
             xi = L["xi"][:, at]
             pad = jnp.zeros((8, tc), F32)
             dxi = ck_ref[3:4, at] * dc
-            rim = jnp.zeros((8, tc), F32)
             vacc[layer, 3:4, at] = jnp.sum(dc * xi[lead:], axis=0, keepdims=True)
             for j in range(3):
                 m = dc * mask[:, j : j + 1]
                 vacc[layer, j : j + 1, at] = jnp.sum(m * xi[lead - 3 + j : lead - 3 + j + t_len], axis=0, keepdims=True)
-                m = m * ck_ref[j : j + 1, at]
-                ext = jnp.concatenate([pad, m, pad], axis=0)
-                dxi = dxi + ext[8 + 3 - j : 8 + 3 - j + t_len]
-                rim = rim + ext[8 - j : 16 - j]
-            deps[:, at] = dxi
-            rims[layer, :, at] = jnp.where(iota((8, tc), 0) < 3, rim, 0.0)
+                ext = jnp.concatenate([m * ck_ref[j : j + 1, at], pad], axis=0)
+                dxi = dxi + ext[3 - j : 3 - j + t_len]
+            dx_both[layer, :, at] = dxi.astype(BF)
+            deps[pl.ds(t_len - BT, BT), at] = dxi[t_len - BT :]
+
+            @pl.when(i == 2 * per_part - 1)
+            def _():
+                @pl.when(me < n - 1)
+                def _():
+                    rim_copy(me).wait_recv()
+
+                add_rim(0)
+
             return carry
 
         lax.fori_loop(0, inner // tc, second, 0)
-
-        def rim_copy(to, layer=layer):
-            return pltpu.make_async_remote_copy(
-                src_ref=rims.at[layer], dst_ref=rimr.at[layer], send_sem=rim_sem.at[layer], recv_sem=rimr_sem.at[layer],
-                device_id=(sec, to), device_id_type=MESH)
-
-        @pl.when(me > 0)
-        def _():
-            rim_copy(me - 1).start()
-
-        @pl.when(me == n - 1)
-        def _():
-            rimr[layer] = jnp.zeros(rimr.shape[1:], F32)
-
+        add_rim(1)
         if layer == 1:
             for name in ("c", "beta", "xi", "y"):
                 load(name, 0).start()
@@ -1376,9 +1399,6 @@
             bufs[layer]["sm"][(1,) + owner(j, bits) + (slice(0, drow),)] = gtmp[j, 0:drow].astype(BF)
         begin(layer, "sm")
         advance(layer, "go")
-        if layer == 0:
-            advance(1, "gx")
-            advance(0, "gz")
         du = jnp.zeros((t_len, width), F32)
 
         def project(du, i, g, layer=layer):
@@ -1394,18 +1414,15 @@
         for i in range(n_in // 2):
             du = project(du, i, dz_ref[:, pl.ds(i * cb, cb)])
 
-        @pl.when(me < n - 1)
-        def _():
-            rim_copy(me).wait_recv()
-
-        tail = jnp.concatenate([jnp.zeros((5, inner), F32), rimr[layer][0:3]], axis=0)
-        deps[pl.ds(t_len - 8, 8), :] = deps[pl.ds(t_len - 8, 8), :] + tail
-        dx_both[layer] = deps[...].astype(BF)
-        ops[layer]["dx0"].send()
-        ops[layer]["dx1"].send()
-        advance(layer, "go", "gz", "sm")
+        if layer == 0:
+            advance(1, "gx", "sm")
+        advance(layer, "gz", "sm")
         for i in range(n_in // 2, n_in):
             du = project(du, i, dx_both[layer, :, pl.ds((i - n_in // 2) * cb, cb)])
+        advance(layer, "go")
+        if layer == 0:
+            advance(1, "gx")
+            advance(0, "gz", "sm")
         load("h", layer).wait()
         hf = L["h"][...].astype(F32)
         inv = lax.rsqrt(jnp.mean(hf * hf, axis=-1, keepdims=True) + NORM_EPS)
@@ -1421,19 +1438,22 @@
         vecs[layer].begin()
 
     parts0 = subs[0]["gx"]
-    advance(0, "sm")
+    half0 = len(parts0) // 2
     grad_gx(0, 0)
-    parts0[0].begin()
-    advance(0, "vec")
+    for s in parts0[:half0]:
+        s.begin()
+    advance(0, "vec", "sm")
     grad_gx(0, 1)
-    parts0[1].begin()
-    parts0[2].begin()
-    advance(0, "gz", "sm")
+    for s in parts0[half0:]:
+        s.begin()
+    advance(0, "go", "gz")
     for _ in range(bits - 1):
-        parts0[0].advance()
-        parts0[2].advance()
-        parts0[1].advance()
-        advance(0, "sm", "vec")
+        for s in parts0[:half0]:
+            s.advance()
+        advance(0, "sm", "go", "gz")
+        for s in parts0[half0:]:
+            s.advance()
+        advance(0, "vec")
     left = [s for layer in range(2) for v in subs[layer].values() for s in v]
     while any(s.stage <= s.last for s in left):
         for s in left[::-1]:
@@ -1514,7 +1534,7 @@
         pltpu.VMEM((2, N, inner), BF), pltpu.VMEM((2, n, N, LANES), BF), pltpu.VMEM((2, n, N, LANES), BF),
         pltpu.VMEM((2, N, inner), BF),
     ]
-    nsub = 1 + 2 + 2 + 3
+    nsub = 1 + 2 + 2 + 4
     dma = pltpu.SemaphoreType.DMA
     scratch += [
         dma((len(LOADS), 2)), dma(()), dma((inner // 512,)), dma((slots,)), dma((2,)), dma((2,)), dma((2,)), dma((2, 2)),

time: 232 us -> 229 us (0.987)
  no operation moved by 1% of the time
where the time goes in v2:
time: 229 us
  Pallas kernels  228 us (100%)
    pallas_call x1, Pallas kernels, backward(): pl.pallas_call(functools.partial(back_kernel, n, rank, {'lead': lead}), o...  151 us
    pallas_call x1, Pallas kernels, forward(): pl.pallas_call(functools.partial(forward_kernel, n, rank), out_shape=outs...  72.3 us

profile of v2, /device:TPU:0, one launch (start us, length us, event | category | flops | bytes accessed | tf_op | source)
XLA Modules:
  0.0 228.6 jit_solution(1856612640615904871)
XLA Ops:
  0.6 72.3 %forward.1 = (bf16[1024,4096]{1,0:T(8,128)(2,1)}, bf16[2048,1024]{1,0:T(8,128)(2,1)}, f32[128,128]{1,0:T(8,128)}, bf16[2,128,2048]{2,1,0:T(8,128)(2,1)}, bf16[2,...) custom-call(s32[2,8]{1,0:T(2,128)} %refs_0_.2, ...), custom_call_target="tpu_custom_call" | custom-call | tf_op jit(solution)/shard_map/forward/pallas_call | solution.py:638
  73.0 151.3 %backward.1 = (bf16[128,1024]{1,0:T(8,128)(2,1)}, f32[64,4096]{1,0:T(8,128)}, f32[128,1024]{1,0:T(8,128)}, f32[2,128,128]{2,1,0:T(8,128)}, f32[16,128]{1,0:T(8,128)}) custom-call(bf16[2,128,1024]{2,1,0:T(8,128)(2,1)} %refs_0_.3, bf16[2,128,1024]{2,1,0:T(8,128)(2,1)} %refs_1_.3, f32[128,128]{1,0:T(8,128)} %get-tuple-element.66.refs_2_, ...), custom_call_target="tpu_custom_call" | custom-call | tf_op jit(solution)/shard_map/backward/pallas_call | solution.py:1545
  224.3 4.1 %finish.1 = (bf16[1,128,1024]{2,1,0:T(8,128)(2,1)}, bf16[1,128,1024]{2,1,0:T(8,128)(2,1)}, f32[1,64]{1,0:T(1,128)}, f32[1,64,4096]{2,1,0:T(8,128)}, f32[1,4,128]...) custom-call(bf16[128,1024]{1,0:T(8,128)(2,1)} %get-tuple-element.65., ...), custom_call_target="tpu_custom_call" | custom-call | tf_op jit(solution)/shard_map/finish/pallas_call | solution.py:1604

commit v3 on v2

--- a/solution.py
+++ b/solution.py
@@ -419,7 +419,7 @@
         keep("k2", layer)
         ec = 512
         nt = ec // LANES
-        un = 8
+        un = 16
         k2_ref, ex_ref, us_ref = loc["k2"], loc["ex"], loc["us"]
 
         def chunk(ci, carry, layer=layer):
@@ -467,10 +467,15 @@
             @pl.when(sec == 0)
             def _():
                 oth(1).start()
+                oth(1).wait_recv()
+                for k in in_order:
+                    in_copy(k, in_oth).start()
 
             @pl.when(sec == 1)
             def _():
                 oth(0).start()
+                oth(0).wait_recv()
+                out_copy(out_oth).start()
         else:
             part_forward(1, 0)
 
@@ -519,18 +524,6 @@
         keep("sb", layer)
         keep("y", layer)
         part_forward(0, layer)
-        if layer == 0:
-            @pl.when(sec == 1)
-            def _():
-                oth(0).wait_recv()
-                out_copy(out_oth).start()
-
-            @pl.when(sec == 0)
-            def _():
-                oth(1).wait_recv()
-                for k in in_order:
-                    in_copy(k, in_oth).start()
-
         out_copy(out_own).wait()
         o = o_all[...]
         hn = (hrow[...].astype(F32) + dot(o, w_out[...])).astype(BF)
@@ -1144,7 +1137,7 @@
         k2_ref, qb_ref, ex_ref = L["k2"], L["qb"], L["ex"]
         ec = 512
         nt = ec // LANES
-        un = 8
+        un = 16
 
         def chunk(ci, carry, k2_ref=k2_ref, qb_ref=qb_ref, ex_ref=ex_ref, layer=layer):
             e0 = pl.multiple_of(ci * ec, ec)

time: 229 us -> 228 us (level)
  no operation moved by 1% of the time
where the time goes in v3:
time: 228 us
  Pallas kernels  227 us (100%)
    pallas_call x1, Pallas kernels, backward(): pl.pallas_call(functools.partial(back_kernel, n, rank, {'lead': lead}), o...  151 us
    pallas_call x1, Pallas kernels, forward(): pl.pallas_call(functools.partial(forward_kernel, n, rank), out_shape=outs...  71.6 us

profile of v3, /device:TPU:0, one launch (start us, length us, event | category | flops | bytes accessed | tf_op | source)
XLA Modules:
  0.0 227.9 jit_solution(15081166655309638252)
XLA Ops:
  0.6 71.6 %forward.1 = (bf16[1024,4096]{1,0:T(8,128)(2,1)}, bf16[2048,1024]{1,0:T(8,128)(2,1)}, f32[128,128]{1,0:T(8,128)}, bf16[2,128,2048]{2,1,0:T(8,128)(2,1)}, bf16[2,...) custom-call(s32[2,8]{1,0:T(2,128)} %refs_0_.2, ...), custom_call_target="tpu_custom_call" | custom-call | tf_op jit(solution)/shard_map/forward/pallas_call | solution.py:631
  72.2 151.3 %backward.1 = (bf16[128,1024]{1,0:T(8,128)(2,1)}, f32[64,4096]{1,0:T(8,128)}, f32[128,1024]{1,0:T(8,128)}, f32[2,128,128]{2,1,0:T(8,128)}, f32[16,128]{1,0:T(8,128)}) custom-call(bf16[2,128,1024]{2,1,0:T(8,128)(2,1)} %refs_0_.3, bf16[2,128,1024]{2,1,0:T(8,128)(2,1)} %refs_1_.3, f32[128,128]{1,0:T(8,128)} %get-tuple-element.66.refs_2_, ...), custom_call_target="tpu_custom_call" | custom-call | tf_op jit(solution)/shard_map/backward/pallas_call | solution.py:1538
  223.6 4.1 %finish.1 = (bf16[1,128,1024]{2,1,0:T(8,128)(2,1)}, bf16[1,128,1024]{2,1,0:T(8,128)(2,1)}, f32[1,64]{1,0:T(1,128)}, f32[1,64,4096]{2,1,0:T(8,128)}, f32[1,4,128]...) custom-call(bf16[128,1024]{1,0:T(8,128)(2,1)} %get-tuple-element.65., ...), custom_call_target="tpu_custom_call" | custom-call | tf_op jit(solution)/shard_map/finish/pallas_call | solution.py:1597
